TPU v7x, 32 devices: a whole 2x2x4 slice. The times are simulated.
32 devices in a mesh: expert: 8 (over z, y), context: 2 (over x), dp: 2 (over core).
Axes of the slice: x: 2, y: 2, z: 4, core: 2. Of those that a mesh axis runs over, the one named last changes fastest.
Arguments:
- tokens: bfloat16 [16, 1024, 768], P(('expert', 'dp'), 'context'), may hold values from -6 to 6
- gain_one: float32 [768], replicated, may hold values from 0.1 to 1.9
- w_qkv: bfloat16 [768, 2304], replicated, may hold values from -0.21875 to 0.21875
- w_out: bfloat16 [768, 768], replicated, may hold values from -6 to 6
- gain_two: float32 [768], replicated, may hold values from 0.1 to 1.9
- w_router: bfloat16 [768, 8], replicated, may hold values from -0.15625 to 0.15625
- w_in: bfloat16 [8, 768, 3072], P('expert'), may hold values from -0.21875 to 0.21875
- w_back: bfloat16 [8, 3072, 768], P('expert'), may hold values from -1.75 to 1.75
- expert_ids: int32 [2, 16, 512, 2], P('context', ('expert', 'dp')), may hold values from 0 to 7, all different within a row; in each aligned block of 512 rows (0 to 511, 512 to 1023, ..., all dimensions but the last counted through in order) at most 256 rows name the same one
- cotangent: bfloat16 [16, 1024, 768], P(('expert', 'dp'), 'context'), may hold values from -6 to 6
Outputs:
- output: bfloat16 [16, 1024, 768], P(('expert', 'dp'), 'context')
- grad_tokens: float32 [16, 1024, 768], P(('expert', 'dp'), 'context')
- grad_gain_one: float32 [768], replicated
- grad_qkv: float32 [768, 2304], replicated
- grad_out: float32 [768, 768], replicated
- grad_gain_two: float32 [768], replicated
- grad_router: float32 [768, 8], replicated
- grad_in: float32 [8, 768, 3072], P('expert', ('context', 'dp'))
- grad_back: float32 [8, 3072, 768], P('expert', ('context', 'dp'))
Inputs may be any that keep to these rules, and one draw needn't show every extreme that they name: `expert_ids`: each token names 2 different experts, numbered by the owner's index along expert. Within the 512 rows of one device (its images of one context index, image by image, in order) no expert is named more than 256 times.
All inputs are finite; a program needn't handle non-finite values.
Results may differ from a plain program's by a relative error of at most 0.017.
Values may be sent and summed in bfloat16 or wider, within the bound.
A program may use at most 256 MiB of HBM per device.

v0:
```python
import jax
import jax.numpy as jnp
from jax import lax
from jax.sharding import PartitionSpec as P

HEADS = 12
HEAD_DIM = 64
TOPK = 2


def layer_norm(values, gain):
    center = jnp.mean(values, axis=-1, keepdims=True)
    shifted = values - center
    variance = jnp.mean(shifted * shifted, axis=-1, keepdims=True)
    return shifted * lax.rsqrt(variance + 1e-06) * gain


def body(tokens, gain_one, w_qkv, w_out, gain_two, w_router, w_in, w_back, expert_ids, cotangent):
    images, tok_ctx, width = tokens.shape
    rows = images * tok_ctx
    experts = lax.axis_size("expert")
    capacity = max(2, 2 * TOPK * rows // experts)
    seq_len = tok_ctx * lax.axis_size("context")
    factor = HEAD_DIM ** (-0.5)
    inputs = tokens.astype(jnp.float32)
    normed, first_back = jax.vjp(layer_norm, inputs, gain_one)
    normed_low = normed.astype(jnp.bfloat16)
    packed = jnp.einsum(
        "isd,de->ise", normed_low, w_qkv, preferred_element_type=jnp.float32
    ).astype(jnp.bfloat16)
    query = packed[..., :width]
    keys_loc = packed[..., width : 2 * width]
    vals_loc = packed[..., 2 * width :]
    keys_all, vals_all = (
        lax.all_gather(keys_loc, "context", axis=1, tiled=True),
        lax.all_gather(vals_loc, "context", axis=1, tiled=True),
    )
    query_h = query.reshape(images, tok_ctx, HEADS, HEAD_DIM)
    keys_h = keys_all.reshape(images, seq_len, HEADS, HEAD_DIM)
    vals_h = vals_all.reshape(images, seq_len, HEADS, HEAD_DIM)
    scores = (
        jnp.einsum("iqhd,ikhd->ihqk", query_h, keys_h, preferred_element_type=jnp.float32) * factor
    )
    peak = jnp.max(scores, axis=-1, keepdims=True)
    expo = jnp.exp(scores - peak)
    totals = jnp.sum(expo, axis=-1, keepdims=True)
    probs = expo / totals
    log_total = peak + jnp.log(totals)
    mixed = jnp.einsum(
        "ihqk,ikhd->iqhd", probs.astype(jnp.bfloat16), vals_h, preferred_element_type=jnp.float32
    )
    mixed_low = mixed.reshape(images, tok_ctx, width).astype(jnp.bfloat16)
    attn_out = jnp.einsum("isd,de->ise", mixed_low, w_out, preferred_element_type=jnp.float32)
    resid = inputs + attn_out
    second, second_back = jax.vjp(layer_norm, resid, gain_two)
    second_low = second.astype(jnp.bfloat16)
    second_rows = second_low.reshape(rows, width)
    logits = jnp.dot(second_rows, w_router, preferred_element_type=jnp.float32)
    gate_probs = jax.nn.softmax(logits, axis=-1)
    routes = expert_ids.reshape(rows, TOPK)
    onehot = (
        routes[..., None] == lax.broadcasted_iota(jnp.int32, (rows, TOPK, experts), 2)
    ).astype(jnp.int32)
    running = jnp.cumsum(onehot.reshape(rows * TOPK, experts), axis=0).reshape(rows, TOPK, experts)
    slot_pos = jnp.sum(running * onehot, axis=-1) - 1
    row_index = lax.broadcasted_iota(jnp.int32, (rows, TOPK), 0)
    table = jnp.zeros((experts, capacity), jnp.int32).at[routes, slot_pos].set(row_index)
    filled = jnp.zeros((experts, capacity), jnp.bfloat16).at[routes, slot_pos].set(1.0)
    onehot_f = onehot.astype(jnp.float32)
    gates = jnp.sum(onehot_f * gate_probs[:, None, :], axis=-1)
    sending = second_rows[table] * filled[..., None]
    weight_in = w_in[0]
    weight_back = w_back[0]
    arrived = lax.all_to_all(sending, "expert", split_axis=0, concat_axis=0, tiled=True)
    hidden = jnp.einsum("sid,df->sif", arrived, weight_in, preferred_element_type=jnp.float32)
    active = jax.nn.gelu(hidden).astype(jnp.bfloat16)
    produced = jnp.einsum(
        "sif,fd->sid", active, weight_back, preferred_element_type=jnp.float32
    ).astype(jnp.bfloat16)
    returned = lax.all_to_all(produced, "expert", split_axis=0, concat_axis=0, tiled=True)
    picked = returned[routes, slot_pos].astype(jnp.float32)
    added = jnp.sum(gates[..., None] * picked, axis=1)
    output = (resid + added.reshape(images, tok_ctx, width)).astype(jnp.bfloat16)
    upstream = cotangent.astype(jnp.float32)
    up_rows = upstream.reshape(rows, width)
    d_gates = jnp.sum(up_rows[:, None, :] * picked, axis=-1)
    slot_grads = (gates[..., None] * up_rows[:, None, :]).astype(jnp.bfloat16)
    grad_buffer = (
        jnp.zeros((experts, capacity, width), jnp.bfloat16).at[routes, slot_pos].set(slot_grads)
    )
    arrived_grad = lax.all_to_all(grad_buffer, "expert", split_axis=0, concat_axis=0, tiled=True)
    active_f, gelu_back = jax.vjp(jax.nn.gelu, hidden)
    active_low = active_f.astype(jnp.bfloat16)
    d_active = jnp.einsum(
        "sid,fd->sif", arrived_grad, weight_back, preferred_element_type=jnp.float32
    )
    d_hidden = gelu_back(d_active)[0].astype(jnp.bfloat16)
    back_part = jnp.einsum(
        "sif,sid->fd", active_low, arrived_grad, preferred_element_type=jnp.float32
    )
    in_part = jnp.einsum("sid,sif->df", arrived, d_hidden, preferred_element_type=jnp.float32)
    d_arrived = jnp.einsum(
        "sif,df->sid", d_hidden, weight_in, preferred_element_type=jnp.float32
    ).astype(jnp.bfloat16)
    returned_grad = lax.all_to_all(d_arrived, "expert", split_axis=0, concat_axis=0, tiled=True)
    d_second = jnp.sum(returned_grad[routes, slot_pos].astype(jnp.float32), axis=1)
    d_probs = jnp.sum(onehot_f * d_gates[..., None], axis=1)
    d_logits = gate_probs * (d_probs - jnp.sum(gate_probs * d_probs, axis=-1, keepdims=True))
    d_logits_low = d_logits.astype(jnp.bfloat16)
    router_part = jnp.dot(second_rows.T, d_logits_low, preferred_element_type=jnp.float32)
    d_second = d_second + jnp.dot(d_logits_low, w_router.T, preferred_element_type=jnp.float32)
    d_resid_norm, gain_two_part = second_back(d_second.reshape(images, tok_ctx, width))
    d_resid = upstream + d_resid_norm
    d_attn = d_resid.astype(jnp.bfloat16)
    out_part = jnp.einsum("isd,ise->de", mixed_low, d_attn, preferred_element_type=jnp.float32)
    d_mixed = jnp.einsum("ise,de->isd", d_attn, w_out, preferred_element_type=jnp.float32).astype(
        jnp.bfloat16
    )
    d_mixed_h = d_mixed.reshape(images, tok_ctx, HEADS, HEAD_DIM)
    probs_again = jnp.exp(
        jnp.einsum("iqhd,ikhd->ihqk", query_h, keys_h, preferred_element_type=jnp.float32) * factor
        - log_total
    )
    d_probs_att = jnp.einsum(
        "iqhd,ikhd->ihqk", d_mixed_h, vals_h, preferred_element_type=jnp.float32
    )
    delta = jnp.sum(probs_again * d_probs_att, axis=-1, keepdims=True)
    d_scores = (factor * probs_again * (d_probs_att - delta)).astype(jnp.bfloat16)
    d_query = jnp.einsum("ihqk,ikhd->iqhd", d_scores, keys_h, preferred_element_type=jnp.float32)
    d_query = d_query.reshape(images, tok_ctx, width).astype(jnp.bfloat16)
    d_keys_all = jnp.einsum(
        "ihqk,iqhd->ikhd", d_scores, query_h, preferred_element_type=jnp.float32
    )
    d_vals_all = jnp.einsum(
        "ihqk,iqhd->ikhd",
        probs_again.astype(jnp.bfloat16),
        d_mixed_h,
        preferred_element_type=jnp.float32,
    )
    d_keys, d_vals = (
        lax.psum_scatter(
            d_keys_all.reshape(images, seq_len, width).astype(jnp.bfloat16),
            "context",
            scatter_dimension=1,
            tiled=True,
        ).astype(jnp.float32),
        lax.psum_scatter(
            d_vals_all.reshape(images, seq_len, width).astype(jnp.bfloat16),
            "context",
            scatter_dimension=1,
            tiled=True,
        ).astype(jnp.float32),
    )
    d_packed = jnp.concatenate(
        [d_query, d_keys.astype(jnp.bfloat16), d_vals.astype(jnp.bfloat16)], axis=-1
    )
    qkv_part = jnp.einsum("isd,ise->de", normed_low, d_packed, preferred_element_type=jnp.float32)
    d_normed = jnp.einsum("ise,de->isd", d_packed, w_qkv, preferred_element_type=jnp.float32)
    d_inputs_norm, gain_one_part = first_back(d_normed)
    grad_tokens = d_resid + d_inputs_norm
    grad_qkv, grad_out, grad_router, grad_gain_one, grad_gain_two = lax.psum(
        (qkv_part, out_part, router_part, gain_one_part, gain_two_part), ("expert", "context", "dp")
    )
    grad_in, grad_back = (
        lax.psum_scatter(
            in_part[None].astype(jnp.bfloat16), ("context", "dp"), scatter_dimension=1, tiled=True
        ).astype(jnp.float32),
        lax.psum_scatter(
            back_part[None].astype(jnp.bfloat16), ("context", "dp"), scatter_dimension=1, tiled=True
        ).astype(jnp.float32),
    )
    return (
        output,
        grad_tokens,
        grad_gain_one,
        grad_qkv,
        grad_out,
        grad_gain_two,
        grad_router,
        grad_in,
        grad_back,
    )


def solution(mesh):
    return jax.shard_map(
        body,
        mesh=mesh,
        in_specs=(
            P(("expert", "dp"), "context", None),
            P(),
            P(),
            P(),
            P(),
            P(),
            P("expert", None, None),
            P("expert", None, None),
            P("context", ("expert", "dp"), None, None),
            P(("expert", "dp"), "context", None),
        ),
        out_specs=(
            P(("expert", "dp"), "context", None),
            P(("expert", "dp"), "context", None),
            P(),
            P(),
            P(),
            P(),
            P(),
            P("expert", ("context", "dp"), None),
            P("expert", ("context", "dp"), None),
        ),
        check_vma=False,
    )
```

profile of v0, /device:TPU:1, one launch (start us, length us, event | category | flops | bytes accessed | tf_op | source)
XLA Modules:
  0.0 999.0 jit_solution(9573434333565673077)
XLA Ops:
  22.4 5.1 reduce-window.6
  47.8 7.9 scatter_custom_fusion.1
  59.0 13.4 %multiply_reduce_fusion.1 = (f32[12,512]{1,0:T(8,128)S(1)}, f32[12,512,1024]{2,1,0:T(8,128)}) fusion(bf16[512,12,64]{0,2,1:T(8,128)(2,1)} %bitcast.168, bf16[1024,12,64]{0,2,1:T(8,128)(2,1)} %bitcast.164), kind=kOutput, calls=%fused_computation.22 | convolution fusion | flops 817883136 | bytes 27549696 | tf_op jit(solution)/shard_map/iqhd,ikhd->ihqk/dot_general | solution.py:42
  73.0 11.6 %fusion.7 = f32[12,512]{1,0:T(8,128)} fusion(f32[12,512,1024]{2,1,0:T(8,128)} %get-tuple-element.33, f32[12,512]{1,0:T(8,128)S(1)} %get-tuple-element.32), kind=kLoop, calls=%fused_computation.21 | loop fusion | flops 18868224 | bytes 25214976 | tf_op jit(solution)/shard_map/reduce_sum | solution.py:46
  87.1 11.5 %fusion.49 = bf16[12,64,512]{2,1,0:T(8,128)(2,1)S(1)} fusion(bf16[1024,12,64]{0,2,1:T(8,128)(2,1)} %bitcast.173, f32[12,512,1024]{2,1,0:T(8,128)} %get-tuple-element.33, f32[12,512]{1,0:T(8,128)} %fusion.7, f32[12,512]{1,0:T(8,128)} %copy-done.18), kind=kOutput, calls=%fused_computation.82 | convolution fusion | flops 830865408 | bytes 27574272 | tf_op jit(solution)/shard_map/ihqk,ikhd->iqhd/dot_general | solution.py:49
  102.5 11.3 %gather_fusion = bf16[2048,768]{1,0:T(8,128)(2,1)} fusion(bf16[512,768]{1,0:T(8,128)(2,1)} %fusion.56, s32[2048]{0:T(1024)S(1)} %broadcast_clamp_fusion), kind=kCustom, calls=%fused_computation | custom fusion | bytes 6299648 | tf_op jit(solution)/shard_map/gather | solution.py:71
  116.0 76.4 %all_to_all.20 = bf16[8,256,768]{2,1,0:T(8,128)(2,1)S(1)} all-to-all(bf16[8,256,768]{2,1,0:T(8,128)(2,1)S(1)} %broadcast_multiply_fusion), channel_id=1, replica_groups=mesh['expert'=8,'context'=2,'dp'=2] {'expert'}, dimensions={0} | all-to-all | bytes 6291456 | tf_op jit(solution)/shard_map/all_to_all | solution.py:74
  192.4 22.5 %multiply_convert_fusion.1 = (bf16[8,256,3072]{2,1,0:T(8,128)(2,1)}, f32[8,256,3072]{2,1,0:T(8,128)}) fusion(bf16[8,256,768]{2,1,0:T(8,128)(2,1)S(1)} %all_to_all.20, bf16[1,768,3072]{2,1,0:T(8,128)(2,1)} %param.16), kind=kOutput, calls=%fused_computation.18 | convolution fusion | flops 9720299520 | bytes 45613056 | tf_op jit(solution)/shard_map/sid,df->sif/dot_general | solution.py:75
  214.9 15.4 %fusion.32 = bf16[8,256,768]{2,1,0:T(8,128)(2,1)} fusion(bf16[8,256,3072]{2,1,0:T(8,128)(2,1)} %get-tuple-element.36, bf16[1,3072,768]{2,1,0:T(8,128)(2,1)} %param.17), kind=kOutput, calls=%fused_computation.56 | convolution fusion | flops 9665249280 | bytes 20447232 | tf_op jit(solution)/shard_map/sif,fd->sid/dot_general | solution.py:77
  242.7 61.2 %all-to-all-done.1 = bf16[8,256,768]{2,1,0:T(8,128)(2,1)} async-done(((bf16[8,256,768]{2,1,0:T(8,128)(2,1)}), bf16[8,256,768]{2,1,0:T(8,128)(2,1)}, u32[]{:S(2)}, u32[]{:S(2)}) %all-to-all-start.1) | async-done | bytes 3145760 | tf_op jit(solution)/shard_map/all_to_all | solution.py:80
  303.9 19.8 %gather_fusion.1 = bf16[1024,768]{1,0:T(8,128)(2,1)} fusion(bf16[8,256,768]{2,1,0:T(8,128)(2,1)} %all-to-all-done.1, s32[1024]{0:T(1024)S(1)} %reshape.437), kind=kCustom, calls=%fused_computation.1 | custom fusion | bytes 3153920 | tf_op jit(solution)/shard_map/gather | solution.py:81
  328.5 12.5 %multiply_reduce_fusion.2 = (f32[512,2]{1,0:T(8,128)}, f32[512,768]{1,0:T(8,128)}, bf16[512,2,768]{2,1,0:T(2,128)(2,1)}) fusion(f32[512,2,768]{2,1,0:T(2,128)} %reshape.469, f32[512,768]{1,0:T(8,128)} %convert_bitcast_fusion, f32[512,2]{1,0:T(8,128)} %copy.85), kind=kLoop, calls=%fused_computation.42 | loop fusion | flops 4324352 | bytes 7872512 | tf_op jit(solution)/shard_map/reduce_sum | solution.py:86
  345.7 7.9 scatter_custom_fusion.2
  353.6 75.7 %all_to_all.21 = bf16[8,256,768]{2,1,0:T(8,128)(2,1)S(1)} all-to-all(bf16[8,256,768]{2,1,0:T(8,128)(2,1)} %bitcast.166), channel_id=1, replica_groups=mesh['expert'=8,'context'=2,'dp'=2] {'expert'}, dimensions={0} | all-to-all | bytes 6291456 | tf_op jit(solution)/shard_map/all_to_all | solution.py:91
  429.3 29.2 %fusion.6 = bf16[8,256,3072]{2,1,0:T(8,128)(2,1)} fusion(f32[8,256,3072]{2,1,0:T(8,128)} %get-tuple-element.37, bf16[8,256,768]{2,1,0:T(8,128)(2,1)S(1)} %all_to_all.21, bf16[1,3072,768]{2,1,0:T(8,128)(2,1)} %param.17), kind=kOutput, calls=%fused_computation.14 | convolution fusion | flops 9789505536 | bytes 45613056 | tf_op jit(solution)/shard_map/sid,fd->sif/dot_general | solution.py:94
  458.6 14.1 %fusion.29 = bf16[8,256,768]{2,1,0:T(8,128)(2,1)} fusion(bf16[8,256,3072]{2,1,0:T(8,128)(2,1)} %fusion.6, bf16[1,768,3072]{2,1,0:T(8,128)(2,1)S(1)} %bitcast.185), kind=kOutput, calls=%fused_computation.55 | convolution fusion | flops 9665249280 | bytes 20447232 | tf_op jit(solution)/shard_map/sif,df->sid/dot_general | solution.py:102
  482.8 63.2 %all-to-all-done.3 = bf16[8,256,768]{2,1,0:T(8,128)(2,1)} async-done(((bf16[8,256,768]{2,1,0:T(8,128)(2,1)}), bf16[8,256,768]{2,1,0:T(8,128)(2,1)}, u32[]{:S(2)}, u32[]{:S(2)}) %all-to-all-start.3) | async-done | bytes 3145760 | tf_op jit(solution)/shard_map/all_to_all | solution.py:105
  546.0 19.7 %gather_fusion.2 = bf16[1024,768]{1,0:T(8,128)(2,1)} fusion(bf16[8,256,768]{2,1,0:T(8,128)(2,1)} %all-to-all-done.3, s32[1024]{0:T(1024)S(1)} %reshape.437), kind=kCustom, calls=%fused_computation.2 | custom fusion | bytes 3153920 | tf_op jit(solution)/shard_map/gather | solution.py:106
  570.5 6.9 reduce_sum.213
  588.8 17.6 %multiply_reduce_fusion = (f32[12,512]{1,0:T(8,128)}, f32[12,512,1024]{2,1,0:T(8,128)}) fusion(f32[12,512,1024]{2,1,0:T(8,128)} %get-tuple-element.33, f32[12,512]{1,0:T(8,128)} %log_add_fusion, bf16[512,12,64]{0,2,1:T(8,128)(2,1)} %bitcast.171, bf16[1024,12,64]{0,2,1:T(8,128)(2,1)} %bitcast.174), kind=kOutput, calls=%fused_computation.16 | convolution fusion | flops 830466048 | bytes 52740096 | tf_op jit(solution)/shard_map/iqhd,ikhd->ihqk/dot_general | solution.py:124
  606.4 17.0 %multiply_convert_fusion = bf16[12,512,1024]{2,1,0:T(8,128)(2,1)S(1)} fusion(f32[12,512,1024]{2,1,0:T(8,128)} %get-tuple-element.42, f32[12,512,1024]{2,1,0:T(8,128)} %get-tuple-element.33, f32[12,512]{1,0:T(8,128)} %get-tuple-element.41, f32[12,512]{1,0:T(8,128)} %log_add_fusion), kind=kLoop, calls=%fused_computation.15 | loop fusion | flops 37748736 | bytes 62963712 | tf_op jit(solution)/shard_map/convert_element_type | solution.py:128
  628.5 12.6 %fusion.37 = bf16[12,64,1024]{2,1,0:T(8,128)(2,1)} fusion(bf16[512,12,64]{0,2,1:T(8,128)(2,1)} %bitcast.172, f32[12,512,1024]{2,1,0:T(8,128)} %get-tuple-element.33, f32[12,512]{1,0:T(8,128)} %log_add_fusion), kind=kOutput, calls=%fused_computation.61 | convolution fusion | flops 824967168 | bytes 27549696 | tf_op jit(solution)/shard_map/ihqk,iqhd->ikhd/dot_general | solution.py:134
  641.2 15.7 %fusion.23 = bf16[1,3072,768]{2,1,0:T(8,128)(2,1)} fusion(bf16[8,256,3072]{2,1,0:T(8,128)(2,1)} %get-tuple-element.36, bf16[8,256,768]{2,1,0:T(8,128)(2,1)} %copy-done.13), kind=kOutput, calls=%fused_computation.39 | convolution fusion | flops 9666035712 | bytes 20447232 | tf_op jit(solution)/shard_map/sif,sid->fd/dot_general | solution.py:98
  657.0 15.4 %fusion.22 = bf16[1,768,3072]{2,1,0:T(8,128)(2,1)} fusion(bf16[8,256,768]{2,1,0:T(8,128)(2,1)} %copy-done.12, bf16[8,256,3072]{2,1,0:T(8,128)(2,1)} %fusion.6), kind=kOutput, calls=%fused_computation.38 | convolution fusion | flops 9666035712 | bytes 20447232 | tf_op jit(solution)/shard_map/sid,sif->df/dot_general | solution.py:101
  676.4 9.4 convolution_convert_fusion.3
  685.9 7.1 fusion.53
  695.1 5.0 fusion.43
  701.6 40.7 %all-reduce = (f32[768]{0:T(1024)}, f32[768]{0:T(1024)}, f32[768,8]{0,1:T(8,128)}) all-reduce(f32[768]{0:T(1024)} %get-tuple-element.13, f32[768]{0:T(1024)} %get-tuple-element.9, f32[768,8]{0,1:T(8,128)} %fusion.82), channel_id=1, replica_groups=mesh['expert'=8,'context'=2,'dp'=2] {'expert','context','dp'}, use_global_device_ids=true, to_apply=%region_28.29 | all-reduce | flops 7680 | bytes 61440 | tf_op jit(solution)/shard_map/psum | solution.py:161
  743.0 4.9 add_add_fusion.2
  750.9 35.2 %reduce-scatter.9.cloned.1.call-done = bf16[1,192,3072]{2,1,0:T(8,128)(2,1)} async-done(((bf16[1,768,3072]{2,1,0:T(8,128)(2,1)}), bf16[1,192,3072]{2,1,0:T(8,128)(2,1)}) %reduce-scatter.9.cloned.1.call-update) | async-done | bytes 1179664 | tf_op jit(solution)/shard_map/reduce_scatter | solution.py:165
  789.0 194.7 %all-reduce.4.cloned.1.call-done = (f32[768,2304]{1,0:T(8,128)}, f32[768,768]{1,0:T(8,128)}) async-done(((f32[768,2304]{1,0:T(8,128)}, f32[768,768]{1,0:T(8,128)}), (f32[768,2304]{1,0:T(8,128)}, f32[768,768]{1,0:T(8,128)})) %all-reduce.4.cloned.1.call-update) | async-done | bytes 9437200 | tf_op jit(solution)/shard_map/psum | solution.py:161
  983.8 6.6 copy.103
  (184 shorter events, 116.7 us)
Async XLA Ops:
  7.2 3.6 copy-start
  7.2 49.1 %all-gather.5.cloned.1.call-start = ((), (), s32[]{:S(2)}) async-start(), calls=%async_computation.9 | async-start | bytes 2359296 | tf_op jit(solution)/shard_map/all_gather | solution.py:35
  8.7 5.4 copy-start.26
  15.6 69.0 %all-gather.3.cloned.1.call-start = ((), (), s32[]{:S(2)}) async-start(), calls=%async_computation.8 | async-start | bytes 2359296 | tf_op jit(solution)/shard_map/all_gather | solution.py:36
  39.0 8.2 copy-start.39
  87.1 11.5 %copy-start.6 = (bf16[1,512,768]{2,1,0:T(8,128)(2,1)S(1)}, bf16[1,512,768]{2,1,0:T(8,128)(2,1)}, u32[]{:S(2)}) copy-start(bf16[1,512,768]{2,1,0:T(8,128)(2,1)} %param.10) | copy-start | bytes 2359300
  87.1 11.5 %copy-start.40 = (bf16[768,768]{1,0:T(8,128)(2,1)S(1)}, bf16[768,768]{1,0:T(8,128)(2,1)}, u32[]{:S(2)}) copy-start(bf16[768,768]{1,0:T(8,128)(2,1)} %param.13) | copy-start | bytes 3538948
  102.5 11.3 %copy-start.38 = (bf16[8,256]{1,0:T(8,128)(2,1)S(1)}, bf16[8,256]{1,0:T(8,128)(2,1)}, u32[]{:S(2)}) copy-start(bf16[8,256]{1,0:T(8,128)(2,1)} %reshape.424) | copy-start | bytes 12292
  192.4 22.5 %copy-start.12 = (bf16[8,256,768]{2,1,0:T(8,128)(2,1)}, bf16[8,256,768]{2,1,0:T(8,128)(2,1)S(1)}, u32[]{:S(2)}) copy-start(bf16[8,256,768]{2,1,0:T(8,128)(2,1)S(1)} %all_to_all.20) | copy-start | bytes 9437188
  230.3 73.6 %all-to-all-start.1 = ((bf16[8,256,768]{2,1,0:T(8,128)(2,1)}), bf16[8,256,768]{2,1,0:T(8,128)(2,1)}, u32[]{:S(2)}, u32[]{:S(2)}) async-start(bf16[8,256,768]{2,1,0:T(8,128)(2,1)} %fusion.32), calls=%async_computation.1 | async-start | bytes 6291456 | tf_op jit(solution)/shard_map/all_to_all | solution.py:80
  240.5 240.8 %copy-start.28 = (f32[512]{0:T(512)}, f32[512]{0:T(512)S(1)}, u32[]{:S(2)}) copy-start(f32[512]{0:T(512)S(1)} %fusion.62) | copy-start | bytes 6148
  353.6 105.0 %slice-start = ((s8[4718592]{0:T(1024)(128)(4,1)}), s8[4194304]{0:T(1024)(128)(4,1)S(1)}, s32[]{:S(2)}) async-start(s8[4718592]{0:T(1024)(128)(4,1)} %bitcast.184), calls=%async_computation.15 | async-start | bytes 8388608
  429.3 29.2 %copy-start.13 = (bf16[8,256,768]{2,1,0:T(8,128)(2,1)}, bf16[8,256,768]{2,1,0:T(8,128)(2,1)S(1)}, u32[]{:S(2)}) copy-start(bf16[8,256,768]{2,1,0:T(8,128)(2,1)S(1)} %all_to_all.21) | copy-start | bytes 9437188
  429.3 29.2 %slice-start.1 = ((s8[4718592]{0:T(1024)(128)(4,1)}), s8[524288]{0:T(1024)(128)(4,1)S(1)}, s32[]{:S(2)}) async-start(s8[4718592]{0:T(1024)(128)(4,1)} %bitcast.184), calls=%async_computation.16 | async-start | bytes 1048576
  472.6 73.3 %all-to-all-start.3 = ((bf16[8,256,768]{2,1,0:T(8,128)(2,1)}), bf16[8,256,768]{2,1,0:T(8,128)(2,1)}, u32[]{:S(2)}, u32[]{:S(2)}) async-start(bf16[8,256,768]{2,1,0:T(8,128)(2,1)} %fusion.29), calls=%async_computation.3 | async-start | bytes 6291456 | tf_op jit(solution)/shard_map/all_to_all | solution.py:105
  477.1 208.7 %reduce-scatter.5.cloned.1.call-start = ((), (), s32[]{:S(2)}) async-start(), calls=%async_computation.10 | async-start | bytes 2359296 | tf_op jit(solution)/shard_map/reduce_scatter | solution.py:141
  570.5 6.9 copy-start.20
  570.5 6.9 copy-start.23
  606.4 17.0 %copy-start.8 = (bf16[1,512,768]{1,2,0:T(8,128)(2,1)S(1)}, bf16[1,512,768]{1,2,0:T(8,128)(2,1)}, u32[]{:S(2)}) copy-start(bf16[1,512,768]{1,2,0:T(8,128)(2,1)} %copy.83) | copy-start | bytes 2359300
  623.4 5.1 copy-start.1
  628.4 57.4 %reduce-scatter.7.cloned.1.call-start = ((), (), s32[]{:S(2)}) async-start(), calls=%async_computation.11 | async-start | bytes 2359296 | tf_op jit(solution)/shard_map/reduce_scatter | solution.py:147
  641.1 106.8 %reduce-scatter.11.cloned.1.call-start = ((), (), s32[]{:S(2)}) async-start(), calls=%async_computation.13 | async-start | bytes 5898240 | tf_op jit(solution)/shard_map/reduce_scatter | solution.py:168
  656.9 129.1 %reduce-scatter.9.cloned.1.call-start = ((), (), s32[]{:S(2)}) async-start(), calls=%async_computation.12 | async-start | bytes 5898240 | tf_op jit(solution)/shard_map/reduce_scatter | solution.py:165
  672.4 311.3 %all-reduce.4.cloned.1.call-start = ((), (), s32[]{:S(2)}) async-start(), calls=%async_computation.14 | async-start | bytes 18874368 | tf_op jit(solution)/shard_map/psum | solution.py:161
  672.7 3.7 copy-start.5
  676.4 9.4 copy-start.25
  676.4 9.4 copy-start.27
  695.1 5.0 copy-start.34
  695.1 5.1 copy-start.7
  695.1 5.1 copy-start.37
  695.1 47.9 %copy-start.32 = (f32[512]{0:T(512)S(1)}, f32[512]{0:T(512)}, u32[]{:S(2)}) copy-start(f32[512]{0:T(512)} %copy-done.31) | copy-start | bytes 6148
  983.8 6.6 copy-start.15
  (21 other events, 38.3 us)
Sparse Core Ops, SparseCore 0:
  15.7 29.2 all-gather.4
  47.2 27.2 all-gather.2
  628.6 27.4 reduce-scatter.4
  658.8 25.9 reduce-scatter.6
  687.2 48.6 reduce-scatter.10
  738.4 47.6 reduce-scatter.8
  792.6 191.1 all-reduce.3
where the time goes:
time: 1010 us; the launch traced here: 999 us
  waiting for transfers between devices  355 us (35%)
  matrix products  210 us (21%)
  blocking collectives  193 us (19%)
  local copies, waits for them, and re-layouts  130 us (13%)
  other arithmetic  86.8 us (9%)
  between operations  15 us (1%)
  starting transfers between devices  10.1 us (1%)
    psum x1, waiting for transfers between devices, body(): lax.psum((qkv_part, out_part, router_part, gain_one_part, gain_two_part),...  195 us
    all_to_all x1, blocking collectives, body(): lax.all_to_all(sending, 'expert', split_axis=0, concat_axis=0, tiled=True)  76.4 us
    all_to_all x1, blocking collectives, body(): lax.all_to_all(grad_buffer, 'expert', split_axis=0, concat_axis=0, tiled=...  75.7 us
    all_to_all x1, waiting for transfers between devices, body(): lax.all_to_all(d_arrived, 'expert', split_axis=0, concat_axis=0, tiled=True)  63.2 us
    all_to_all x1, waiting for transfers between devices, body(): lax.all_to_all(produced, 'expert', split_axis=0, concat_axis=0, tiled=True)  61.2 us
    psum x1, blocking collectives, body(): lax.psum((qkv_part, out_part, router_part, gain_one_part, gain_two_part),...  40.7 us
    unnamed x98, local copies, waits for them, and re-layouts  38.1 us
    reduce_scatter x1, waiting for transfers between devices, body(): lax.psum_scatter(in_part[None].astype(jnp.bfloat16), ('context', 'dp'), s...  35.2 us
  transfers between devices with their start and end apart: 9, of which 4 were waited for; matrix products, arithmetic and copies ran while one was open for 16% of the time, Pallas kernels for 0%

commit v1 on v0

v1 whole, which is shorter than its diff:
```python
import functools

import jax
import jax.numpy as jnp
from jax import lax
from jax.experimental import pallas as pl
from jax.experimental.pallas import tpu as pltpu
from jax.sharding import PartitionSpec as P

HEADS = 12
HEAD_DIM = 64
TOPK = 2
PAIR = 2 * HEAD_DIM
FACTOR = HEAD_DIM ** (-0.5)
LOW = jnp.bfloat16
FULL = jnp.float32
EVERY = ("expert", "context", "dp")
VMEM_LIMIT = 56 * 1024 * 1024


def layer_norm(values, gain):
    center = jnp.mean(values, axis=-1, keepdims=True)
    shifted = values - center
    variance = jnp.mean(shifted * shifted, axis=-1, keepdims=True)
    return shifted * lax.rsqrt(variance + 1e-06) * gain


def contract(left, right, left_dim, right_dim):
    return lax.dot_general(
        left, right, (((left_dim,), (right_dim,)), ((), ())), preferred_element_type=FULL
    )


def attend_kernel(query_ref, keys_ref, vals_ref, mixed_ref, lse_ref):
    parts = []
    for half in range(2):
        cols = slice(half * HEAD_DIM, (half + 1) * HEAD_DIM)
        query = query_ref[0, :, cols] * LOW(FACTOR)
        scores = contract(keys_ref[0, :, cols], query, 1, 1)
        peak = jnp.max(scores, axis=0, keepdims=True)
        expo = jnp.exp(scores - peak)
        total = jnp.sum(expo, axis=0, keepdims=True)
        lse_ref[0, 0, half : half + 1, :] = peak + jnp.log(total)
        parts.append(contract(vals_ref[0, :, cols], expo.astype(LOW), 0, 0) / total)
    mixed_ref[0] = jnp.concatenate(parts, axis=0).T.astype(LOW)


def attend(query, keys, vals):
    images, tok, width = query.shape
    seq = keys.shape[1]
    pairs = width // PAIR
    near = pl.BlockSpec((1, tok, PAIR), lambda i, p: (i, 0, p))
    whole = pl.BlockSpec((1, seq, PAIR), lambda i, p: (i, 0, p))
    return pl.pallas_call(
        attend_kernel,
        grid=(images, pairs),
        in_specs=[near, whole, whole],
        out_specs=[near, pl.BlockSpec((1, 1, 2, tok), lambda i, p: (i, p, 0, 0))],
        out_shape=[
            jax.ShapeDtypeStruct((images, tok, width), LOW),
            jax.ShapeDtypeStruct((images, pairs, 2, tok), FULL),
        ],
        compiler_params=pltpu.CompilerParams(vmem_limit_bytes=VMEM_LIMIT),
        cost_estimate=pl.CostEstimate(
            flops=4 * images * tok * seq * width,
            bytes_accessed=4 * images * (tok + seq) * width,
            transcendentals=images * tok * seq * HEADS,
        ),
        name="attend",
    )(query, keys, vals)


def attend_back_kernel(
    query_ref, keys_ref, vals_ref, up_ref, lse_ref, d_query_ref, d_keys_ref, d_vals_ref
):
    parts = []
    for half in range(2):
        cols = slice(half * HEAD_DIM, (half + 1) * HEAD_DIM)
        query = query_ref[0, :, cols] * LOW(FACTOR)
        keys = keys_ref[0, :, cols]
        up = up_ref[0, :, cols]
        probs = jnp.exp(contract(keys, query, 1, 1) - lse_ref[0, 0, half : half + 1, :])
        d_probs = contract(vals_ref[0, :, cols], up, 1, 1)
        delta = jnp.sum(probs * d_probs, axis=0, keepdims=True)
        d_scores = (probs * (d_probs - delta)).astype(LOW)
        d_vals_ref[0, :, cols] = contract(probs.astype(LOW), up, 1, 0).astype(LOW)
        d_keys_ref[0, :, cols] = contract(d_scores, query, 1, 0).astype(LOW)
        parts.append(contract(keys, d_scores, 0, 0) * FACTOR)
    d_query_ref[0] = jnp.concatenate(parts, axis=0).T.astype(LOW)


def attend_back(query, keys, vals, up, lse):
    images, tok, width = query.shape
    seq = keys.shape[1]
    pairs = width // PAIR
    near = pl.BlockSpec((1, tok, PAIR), lambda i, p: (i, 0, p))
    whole = pl.BlockSpec((1, seq, PAIR), lambda i, p: (i, 0, p))
    return pl.pallas_call(
        attend_back_kernel,
        grid=(images, pairs),
        in_specs=[near, whole, whole, near, pl.BlockSpec((1, 1, 2, tok), lambda i, p: (i, p, 0, 0))],
        out_specs=[near, whole, whole],
        out_shape=[
            jax.ShapeDtypeStruct((images, tok, width), LOW),
            jax.ShapeDtypeStruct((images, seq, width), LOW),
            jax.ShapeDtypeStruct((images, seq, width), LOW),
        ],
        compiler_params=pltpu.CompilerParams(vmem_limit_bytes=VMEM_LIMIT),
        cost_estimate=pl.CostEstimate(
            flops=10 * images * tok * seq * width,
            bytes_accessed=8 * images * (tok + seq) * width,
            transcendentals=images * tok * seq * HEADS,
        ),
        name="attend_back",
    )(query, keys, vals, up, lse)


def partners(axis, shift):
    return [(i, i ^ shift) for i in range(lax.axis_size(axis))]


def swap(block, axis, shift):
    return lax.ppermute(block, axis, partners(axis, shift)) if shift else block


def gather_near_first(block, axis):
    return [swap(block, axis, shift) for shift in range(lax.axis_size(axis))]


def scatter_sum(block, axis):
    size = block.shape[0] // lax.axis_size(axis)
    me = lax.axis_index(axis)
    total = None
    for shift in range(lax.axis_size(axis)):
        piece = lax.dynamic_slice_in_dim(block, (me ^ shift) * size, size, 0)
        piece = swap(piece, axis, shift).astype(FULL)
        total = piece if total is None else total + piece
    return total.astype(LOW)


def gather_in_order(block, axis):
    size = block.shape[0]
    me = lax.axis_index(axis)
    out = jnp.zeros((size * lax.axis_size(axis),) + block.shape[1:], block.dtype)
    for shift, piece in enumerate(gather_near_first(block, axis)):
        out = lax.dynamic_update_slice_in_dim(out, piece, (me ^ shift) * size, 0)
    return out


def sum_everywhere(part, order):
    high, wide = part.shape
    value = part.astype(LOW).reshape(high, 2, wide // 2).transpose(1, 0, 2)
    value = value.reshape(2 * high, wide // 2)
    for axis in order:
        value = scatter_sum(value, axis)
    for axis in order[::-1]:
        value = gather_in_order(value, axis)
    return value.reshape(2, high, wide // 2).transpose(1, 0, 2).reshape(high, wide).astype(FULL)


def expert_rows(arrived, up, w_router, weight_in, weight_back, mine):
    gate_probs = jax.nn.softmax(
        jnp.dot(arrived, w_router, preferred_element_type=FULL), axis=-1
    )
    column = (lax.broadcasted_iota(jnp.int32, gate_probs.shape, 1) == mine).astype(FULL)
    gate = jnp.sum(gate_probs * column, axis=-1, keepdims=True)
    hidden = jnp.dot(arrived, weight_in, preferred_element_type=FULL)
    active, gelu_back = jax.vjp(jax.nn.gelu, hidden)
    active_low = active.astype(LOW)
    produced = jnp.dot(active_low, weight_back, preferred_element_type=FULL)
    up_full = up.astype(FULL)
    d_gate = jnp.sum(up_full * produced, axis=-1)
    gated = (gate * produced).astype(LOW)
    d_produced = (gate * up_full).astype(LOW)
    d_active = contract(d_produced, weight_back, 1, 1)
    d_hidden = gelu_back(d_active)[0].astype(LOW)
    d_arrived = contract(d_hidden, weight_in, 1, 1).astype(LOW)
    return active_low, d_produced, d_hidden, gated, d_gate, d_arrived


def body(tokens, gain_one, w_qkv, w_out, gain_two, w_router, w_in, w_back, expert_ids, cotangent):
    images, tok_ctx, width = tokens.shape
    rows = images * tok_ctx
    experts = lax.axis_size("expert")
    mine = lax.axis_index("expert")
    capacity = max(2, 2 * TOPK * rows // experts)
    weight_in = w_in[0]
    weight_back = w_back[0]

    tokens_img = jnp.concatenate(gather_near_first(tokens, "context"), axis=1)

    routes = expert_ids.reshape(rows, TOPK).T
    owners = mine ^ lax.broadcasted_iota(jnp.int32, (experts, 1), 0)
    named = (routes[0][None] == owners) | (routes[1][None] == owners)
    place = jnp.where(named, jnp.cumsum(named.astype(jnp.int32), axis=1) - 1, -1)
    choose = (
        place[:, None, :] == lax.broadcasted_iota(jnp.int32, (experts, capacity, rows), 1)
    ).astype(LOW)
    far = experts // 2
    groups = (range(far), range(far, experts))

    def dispatch(values, group):
        chosen = choose[group.start : group.stop].reshape(-1, rows)
        sent = jnp.dot(chosen, values, preferred_element_type=FULL).astype(LOW)
        return [
            swap(sent[n * capacity : (n + 1) * capacity], "expert", shift)
            for n, shift in enumerate(group)
        ]

    def send_back(values, group):
        return [
            swap(values[n * capacity : (n + 1) * capacity], "expert", shift)
            for n, shift in enumerate(group)
        ]

    def collect(pieces):
        return contract(choose.reshape(-1, rows), jnp.concatenate(pieces, axis=0), 0, 0)

    up_rows = cotangent.reshape(rows, width)
    up_far = jnp.concatenate(dispatch(up_rows, groups[1]), axis=0)
    up_near = jnp.concatenate(dispatch(up_rows, groups[0]), axis=0)

    inputs = tokens.astype(FULL)
    normed, first_back = jax.vjp(layer_norm, inputs, gain_one)
    normed_low = normed.astype(LOW)
    query = jnp.einsum(
        "isd,de->ise", normed_low, w_qkv[:, :width], preferred_element_type=FULL
    ).astype(LOW)
    normed_img = layer_norm(tokens_img.astype(FULL), gain_one).astype(LOW)
    keys = jnp.einsum(
        "isd,de->ise", normed_img, w_qkv[:, width : 2 * width], preferred_element_type=FULL
    ).astype(LOW)
    vals = jnp.einsum(
        "isd,de->ise", normed_img, w_qkv[:, 2 * width :], preferred_element_type=FULL
    ).astype(LOW)
    mixed_low, lse = attend(query, keys, vals)
    attn_out = jnp.einsum("isd,de->ise", mixed_low, w_out, preferred_element_type=FULL)
    resid = inputs + attn_out
    second, second_back = jax.vjp(layer_norm, resid, gain_two)
    second_rows = second.astype(LOW).reshape(rows, width)

    arrived_far = jnp.concatenate(dispatch(second_rows, groups[1]), axis=0)
    arrived_near = jnp.concatenate(dispatch(second_rows, groups[0]), axis=0)
    act_n, dp_n, dh_n, gated_n, dg_n, da_n = expert_rows(
        arrived_near, up_near, w_router, weight_in, weight_back, mine
    )
    act_f, dp_f, dh_f, gated_f, dg_f, da_f = expert_rows(
        arrived_far, up_far, w_router, weight_in, weight_back, mine
    )
    d_rows_near = send_back(da_n, groups[0])
    d_rows_far = send_back(da_f, groups[1])
    d_gate_back = [
        swap(piece, "expert", shift)
        for shift, piece in enumerate(
            jnp.concatenate([dg_n, dg_f]).reshape(experts, -1, 128)
        )
    ]
    back_part = contract(act_n, dp_n, 0, 0) + contract(act_f, dp_f, 0, 0)
    in_part = contract(arrived_near, dh_n, 0, 0) + contract(arrived_far, dh_f, 0, 0)

    d_rows = collect(d_rows_near + d_rows_far)
    gated_f, gated_n, d_rows = lax.optimization_barrier((gated_f, gated_n, d_rows))
    added = collect(send_back(gated_n, groups[0]) + send_back(gated_f, groups[1]))
    output = (resid + added.reshape(images, tok_ctx, width)).astype(LOW)
    gate_probs = jax.nn.softmax(
        jnp.dot(second_rows, w_router, preferred_element_type=FULL), axis=-1
    )
    d_gate_slots = jnp.stack(d_gate_back).reshape(experts, capacity)
    d_gate_tok = jnp.sum(choose.astype(FULL) * d_gate_slots[:, :, None], axis=1)
    to_column = (owners == lax.broadcasted_iota(jnp.int32, (experts, experts), 1)).astype(FULL)
    d_probs = jnp.sum(d_gate_tok[:, :, None] * to_column[:, None, :], axis=0)
    d_logits = gate_probs * (d_probs - jnp.sum(gate_probs * d_probs, axis=-1, keepdims=True))
    d_logits_low = d_logits.astype(LOW)
    router_part = contract(second_rows, d_logits_low, 0, 0)
    d_second = d_rows + contract(d_logits_low, w_router, 1, 1)
    d_resid_norm, gain_two_part = second_back(d_second.reshape(images, tok_ctx, width))
    d_resid = cotangent.astype(FULL) + d_resid_norm
    d_attn = d_resid.astype(LOW)
    grad_of = functools.partial(jnp.einsum, "isd,ise->de", preferred_element_type=FULL)
    d_mixed = jnp.einsum("ise,de->isd", d_attn, w_out, preferred_element_type=FULL).astype(LOW)

    d_query, d_keys_img, d_vals_img = attend_back(query, keys, vals, d_mixed, lse)

    def sum_context(part):
        total = None
        for shift in range(lax.axis_size("context")):
            piece = swap(part[:, shift * tok_ctx : (shift + 1) * tok_ctx], "context", shift)
            total = piece.astype(FULL) if total is None else total + piece.astype(FULL)
        return total.astype(LOW)

    d_keys = sum_context(d_keys_img)
    d_vals = sum_context(d_vals_img)
    grad_out = sum_everywhere(grad_of(mixed_low, d_attn), ("dp", "context", "expert"))
    grad_v = sum_everywhere(grad_of(normed_img, d_vals_img), ("dp", "context", "expert"))
    grad_k = sum_everywhere(grad_of(normed_img, d_keys_img), ("dp", "expert", "context"))
    grad_q = sum_everywhere(grad_of(normed_low, d_query), ("context", "dp", "expert"))
    d_packed = jnp.concatenate([d_query, d_keys, d_vals], axis=-1)
    d_normed = jnp.einsum("ise,de->isd", d_packed, w_qkv, preferred_element_type=FULL)
    d_inputs_norm, gain_one_part = first_back(d_normed)
    grad_tokens = d_resid + d_inputs_norm
    grad_router, grad_gain_one, grad_gain_two = lax.psum(
        (router_part, gain_one_part, gain_two_part), EVERY
    )
    grad_in, grad_back = (
        lax.psum_scatter(
            part[None].astype(LOW), ("context", "dp"), scatter_dimension=1, tiled=True
        ).astype(FULL)
        for part in (in_part, back_part)
    )
    return (
        output,
        grad_tokens,
        grad_gain_one,
        jnp.concatenate([grad_q, grad_k, grad_v], axis=-1),
        grad_out,
        grad_gain_two,
        grad_router,
        grad_in,
        grad_back,
    )


def solution(mesh):
    return jax.shard_map(
        body,
        mesh=mesh,
        in_specs=(
            P(("expert", "dp"), "context", None),
            P(),
            P(),
            P(),
            P(),
            P(),
            P("expert", None, None),
            P("expert", None, None),
            P("context", ("expert", "dp"), None, None),
            P(("expert", "dp"), "context", None),
        ),
        out_specs=(
            P(("expert", "dp"), "context", None),
            P(("expert", "dp"), "context", None),
            P(),
            P(),
            P(),
            P(),
            P(),
            P("expert", ("context", "dp"), None),
            P("expert", ("context", "dp"), None),
        ),
        check_vma=False,
    )
```

time: 1010 us -> 826 us (0.82)
  starting transfers between devices: 10.1 us -> 216 us
  waiting for transfers between devices: 355 us -> 183 us
  blocking collectives: 193 us -> 45.4 us
  other arithmetic: 86.8 us -> 32.8 us
  Pallas kernels: 0 us -> 36.4 us
  matrix products: 210 us -> 178 us
  local copies, waits for them, and re-layouts: 130 us -> 108 us
    ppermute x0 -> x110, starting transfers between devices: none -> 216 us  [swap(): return lax.ppermute(block, axis, partners(axis, shift)) if shift else block]
    psum x1 -> x0, waiting for transfers between devices: 195 us -> none  [body(): lax.psum((qkv_part, out_part, router_part, gain_one_part, gain_two_part),...]
    ppermute x0 -> x110, waiting for transfers between devices: none -> 183 us  [swap(): return lax.ppermute(block, axis, partners(axis, shift)) if shift else block]
    all_to_all x2 -> x0, blocking collectives: 152 us -> none  [the longest x1 76.4 us: body(): lax.all_to_all(sending, 'expert', split_axis=0, concat_axis=0, tiled=True)]
    all_to_all x2 -> x0, waiting for transfers between devices: 124 us -> none  [the longest x1 63.2 us: body(): lax.all_to_all(d_arrived, 'expert', split_axis=0, concat_axis=0, tiled=True)]
    gather x3 -> x0, local copies, waits for them, and re-layouts: 50.8 us -> none  [the longest x1 19.8 us: body(): picked = returned[routes, slot_pos].astype(jnp.float32)]
    pallas_call x0 -> x2, Pallas kernels: none -> 36.4 us  [the longest x1 22.2 us: attend_back(): pl.pallas_call(attend_back_kernel, grid=(images, pairs), in_specs=[near,...]
    reduce_scatter x4 -> x2, waiting for transfers between devices: 35.2 us -> 0.01 us  [body(): lax.psum_scatter(part[None].astype(LOW), ('context', 'dp'), scatter_dimen...]
  transfers between devices with their start and end apart: 9 -> 112, of which waited for: 4 -> 17; matrix products, arithmetic and copies ran while one was open for 16% -> 34% of each run, Pallas kernels for 0% -> 4%
where the time goes in v1:
time: 826 us; the launch traced here: 816 us
  starting transfers between devices  216 us (26%)
  waiting for transfers between devices  183 us (22%)
  matrix products  178 us (22%)
  local copies, waits for them, and re-layouts  108 us (13%)
  blocking collectives  45.4 us (5%)
  Pallas kernels  36.4 us (4%)
  other arithmetic  32.8 us (4%)
  between operations  16.2 us (2%)
    ppermute x110, starting transfers between devices, swap(): return lax.ppermute(block, axis, partners(axis, shift)) if shift else block  216 us
    ppermute x110, waiting for transfers between devices, swap(): return lax.ppermute(block, axis, partners(axis, shift)) if shift else block  183 us
    dot_general x12, matrix products, contract(): lax.dot_general(left, right, (((left_dim,), (right_dim,)), ((), ())), pre...  101 us
    psum x1, blocking collectives, body(): lax.psum((router_part, gain_one_part, gain_two_part), EVERY)  45.4 us
    unnamed x239, local copies, waits for them, and re-layouts  37.4 us
    dot_general x2, matrix products, expert_rows(): produced = jnp.dot(active_low, weight_back, preferred_element_type=FULL)  25 us
    pallas_call x1, Pallas kernels, attend_back(): pl.pallas_call(attend_back_kernel, grid=(images, pairs), in_specs=[near,...  22.2 us
    dynamic_update_slice x44, local copies, waits for them, and re-layouts, gather_in_order(): out = lax.dynamic_update_slice_in_dim(out, piece, (me ^ shift) * size, 0)  21.2 us
  transfers between devices with their start and end apart: 112, of which 17 were waited for; matrix products, arithmetic and copies ran while one was open for 34% of the time, Pallas kernels for 4%

profile of v1, /device:TPU:1, one launch (start us, length us, event | category | flops | bytes accessed | tf_op | source)
XLA Modules:
  0.0 816.4 jit_solution(9869933682979204927)
XLA Ops:
  38.4 14.2 %attend.1 = (bf16[1,512,768]{2,1,0:T(8,128)(2,1)}, f32[1,6,2,512]{3,2,1,0:T(2,128)}) custom-call(bf16[1,512,768]{2,1,0:T(8,128)(2,1)} %fusion.83.query_ref, bf16[1,1024,768]{2,1,0:T(8,128)(2,1)} %fusion.76.keys_ref, bf16[1,1024,768]{2,1,0:T(8,128)(2,1)} %fusion.77.vals_ref), custom_call_target="tpu_custom_call" | custom-call | flops 1610612736 | bytes 4718592 | tf_op jit(solution)/shard_map/attend/pallas_call | solution.py:54
  66.6 36.9 %collective-permute-done.1 = bf16[256,768]{1,0:T(8,128)(2,1)S(1)} collective-permute-done((bf16[256,768]{1,0:T(8,128)(2,1)S(1)}, bf16[256,768]{1,0:T(8,128)(2,1)S(1)}, u32[]{:S(2)}, u32[]{:S(2)}) %collective-permute-start.1) | collective-permute-done | bytes 393248 | tf_op jit(solution)/shard_map/ppermute | solution.py:123
  103.8 17.6 %collective-permute-done.2 = bf16[256,768]{1,0:T(8,128)(2,1)S(1)} collective-permute-done((bf16[256,768]{1,0:T(8,128)(2,1)S(1)}, bf16[256,768]{1,0:T(8,128)(2,1)S(1)}, u32[]{:S(2)}, u32[]{:S(2)}) %collective-permute-start.2) | collective-permute-done | bytes 393248 | tf_op jit(solution)/shard_map/ppermute | solution.py:123
  121.6 7.5 collective-permute-start.6
  129.1 9.3 %collective-permute-start.7 = (bf16[256,768]{1,0:T(8,128)(2,1)S(1)}, bf16[256,768]{1,0:T(8,128)(2,1)S(1)}, u32[]{:S(2)}, u32[]{:S(2)}) collective-permute-start(bf16[256,768]{1,0:T(8,128)(2,1)S(1)} %get-tuple-element.91), channel_id=1, source_target_pairs={{0,12},{4,8},{8,4},{12,0},{16,28},{20,24},{24,20},{28,16},{1,13},{... | collective-permute-start | bytes 1179656 | tf_op jit(solution)/shard_map/ppermute | solution.py:123
  138.6 7.9 fusion.28
  151.3 21.4 %collective-permute-done.7 = bf16[256,768]{1,0:T(8,128)(2,1)S(1)} collective-permute-done((bf16[256,768]{1,0:T(8,128)(2,1)S(1)}, bf16[256,768]{1,0:T(8,128)(2,1)S(1)}, u32[]{:S(2)}, u32[]{:S(2)}) %collective-permute-start.7) | collective-permute-done | bytes 393248 | tf_op jit(solution)/shard_map/ppermute | solution.py:123
  177.2 17.5 %fusion.6 = bf16[1024,3072]{1,0:T(8,128)(2,1)} fusion(f32[1024,3072]{1,0:T(8,128)} %fusion.28, bf16[1,3072,768]{2,1,0:T(8,128)(2,1)S(1)} %bitcast.253, f32[1024]{0:T(1024)S(1)} %get-tuple-element.48, bf16[256,768]{0,1:T(8,128)(2,1)S(1)} %collective-permute-done.17, bf16[256,768]{0,1:T(8,128)(2,1)S(1)} %collective-permute-done.16, ...), kind=kOutput, calls=%fused_computation.10 | convolution fusion | flops 4902617088 | bytes 25169920 | tf_op jit(solution)/shard_map/dot_general | solution.py:29
  194.7 7.9 fusion.126
  202.6 11.9 %fusion.26 = f32[1024,3072]{1,0:T(8,128)} fusion(bf16[1,768,3072]{2,1,0:T(8,128)(2,1)} %param.16, bf16[256,768]{1,0:T(8,128)(2,1)S(1)} %copy-done.54, bf16[256,768]{1,0:T(8,128)(2,1)S(1)} %copy-done.52, bf16[256,768]{1,0:T(8,128)(2,1)S(1)} %copy-done.50, bf16[256,768]{1,0:T(8,128)(2,1)S(1)} %get-tuple-element.90), kind=kOutput, calls=%fused_computation.34 | convolution fusion | flops 4838129664 | bytes 18874368 | tf_op jit(solution)/shard_map/dot_general | solution.py:167
  214.5 18.6 %fusion.13 = bf16[1024,3072]{1,0:T(8,128)(2,1)} fusion(f32[1024,3072]{1,0:T(8,128)} %fusion.26, bf16[1,3072,768]{2,1,0:T(8,128)(2,1)} %param.17, f32[1024]{0:T(1024)S(1)} %get-tuple-element.47, bf16[256,768]{0,1:T(8,128)(2,1)} %collective-permute-done.10, bf16[256,768]{0,1:T(8,128)(2,1)} %collective-permute-done.9, ...), kind=kOutput, calls=%fused_computation.17 | convolution fusion | flops 4902617088 | bytes 25169920 | tf_op jit(solution)/shard_map/dot_general | solution.py:29
  233.2 9.3 %fusion.30 = bf16[1,768,3072]{2,1,0:T(8,128)(2,1)} fusion(f32[768,3072]{1,0:T(8,128)S(1)} %fusion.126, bf16[1024,3072]{1,0:T(8,128)(2,1)} %fusion.13, bf16[256,768]{1,0:T(8,128)(2,1)} %copy-done.53, bf16[256,768]{1,0:T(8,128)(2,1)} %copy-done.51, bf16[256,768]{1,0:T(8,128)(2,1)} %copy-done.49, bf16[256,768]{1,0:T(8,128)(2,1)S(1)} %get-tuple-element.90), kind=kOutput, calls=%fused_computation.38 | convolution fusion | flops 4842848256 | bytes 22020096 | tf_op jit(solution)/shard_map/dot_general | solution.py:29
  242.6 12.5 %fusion.35 = (f32[1024]{0:T(1024)S(1)}, bf16[1024,768]{0,1:T(8,128)(2,1)}) fusion(bf16[256,768]{0,1:T(8,128)(2,1)} %collective-permute-done.10, bf16[256,768]{0,1:T(8,128)(2,1)} %collective-permute-done.9, bf16[256,768]{0,1:T(8,128)(2,1)} %collective-permute-done.8, bf16[256,768]{0,1:T(8,128)(2,1)S(1)} %copy-done.43, f32[1024]{0:T(1024)S(1)} %get-tuple-element.47, ...), kind=kOutput, calls=%fused_computation.53 | convolution fusion | flops 4869585920 | bytes 20455424 | tf_op jit(solution)/shard_map/dot_general | solution.py:170
  256.4 9.7 %collective-permute-start.30 = (f32[2,128]{1,0:T(2,128)S(1)}, f32[2,128]{1,0:T(2,128)S(1)}, u32[]{:S(2)}, u32[]{:S(2)}) collective-permute-start(f32[2,128]{1,0:T(2,128)S(1)} %get-tuple-element.133), channel_id=1, source_target_pairs={{0,8},{4,12},{8,0},{12,4},{16,24},{20,28},{24,16},{28,20},{1,9},{5... | collective-permute-start | bytes 3080 | tf_op jit(solution)/shard_map/ppermute | solution.py:123
  266.2 12.5 %fusion.37 = (f32[1024]{0:T(1024)S(1)}, bf16[1024,768]{0,1:T(8,128)(2,1)}) fusion(bf16[256,768]{0,1:T(8,128)(2,1)S(1)} %copy-done.96, bf16[256,768]{0,1:T(8,128)(2,1)S(1)} %copy-done.93, bf16[256,768]{0,1:T(8,128)(2,1)S(1)} %copy-done.90, bf16[256,768]{0,1:T(8,128)(2,1)} %collective-permute-done.14, f32[1024]{0:T(1024)S(1)} %get-tuple-element.48, ...), kind=kOutput, calls=%fused_computation.55 | convolution fusion | flops 4869585920 | bytes 20455424 | tf_op jit(solution)/shard_map/dot_general | solution.py:170
  284.3 6.6 fusion.54
  296.1 11.9 %fusion.80 = f32[3072,768]{1,0:T(8,128)S(1)} fusion(f32[1024]{0:T(1024)S(1)} %get-tuple-element.47, bf16[256,768]{0,1:T(8,128)(2,1)} %collective-permute-done.10, bf16[256,768]{0,1:T(8,128)(2,1)} %collective-permute-done.9, bf16[256,768]{0,1:T(8,128)(2,1)} %collective-permute-done.8, bf16[256,768]{0,1:T(8,128)(2,1)S(1)} %copy-done.43, f32[1024,3072]{1,0:T(8,128)} %fusion.26), kind=kOutput, calls=%fused_computation.119 | convolution fusion | flops 4868014080 | bytes 23597056 | tf_op jit(solution)/shard_map/dot_general | solution.py:29
  308.0 13.1 %fusion.31 = bf16[1,3072,768]{2,1,0:T(8,128)(2,1)} fusion(f32[3072,768]{1,0:T(8,128)S(1)} %fusion.80, f32[1024]{0:T(1024)S(1)} %get-tuple-element.48, bf16[256,768]{0,1:T(8,128)(2,1)S(1)} %copy-done.97, bf16[256,768]{0,1:T(8,128)(2,1)S(1)} %copy-done.94, bf16[256,768]{0,1:T(8,128)(2,1)S(1)} %copy-done.91, bf16[256,768]{0,1:T(8,128)(2,1)} %collective-permute-done.14, ...), kind=kOutput, calls=%fused_computation.39 | convolution fusion | flops 4872732672 | bytes 28315648 | tf_op jit(solution)/shard_map/dot_general | solution.py:29
  347.8 12.5 %collective-permute-done.13 = bf16[256,768]{1,0:T(8,128)(2,1)} collective-permute-done((bf16[256,768]{1,0:T(8,128)(2,1)}, bf16[256,768]{1,0:T(8,128)(2,1)}, u32[]{:S(2)}, u32[]{:S(2)}) %collective-permute-start.13) | collective-permute-done | bytes 393248 | tf_op jit(solution)/shard_map/ppermute | solution.py:123
  368.5 8.5 %collective-permute-done.21 = bf16[256,768]{1,0:T(8,128)(2,1)S(1)} collective-permute-done((bf16[256,768]{1,0:T(8,128)(2,1)S(1)}, bf16[256,768]{1,0:T(8,128)(2,1)S(1)}, u32[]{:S(2)}, u32[]{:S(2)}) %collective-permute-start.21) | collective-permute-done | bytes 393248 | tf_op jit(solution)/shard_map/ppermute | solution.py:123
  393.6 12.7 %collective-permute-start.92 = (bf16[768,384]{1,0:T(8,128)(2,1)}, bf16[768,384]{1,0:T(8,128)(2,1)}, u32[]{:S(2)}, u32[]{:S(2)}) collective-permute-start(bf16[768,384]{1,0:T(8,128)(2,1)} %constant_dynamic-slice_fusion.8), channel_id=1, source_target_pairs={{0,1},{1,0},{2,3},{3,2},{4,5},{5,4},{6,7},{7,6},{8,9},{9,8},{10,11... | collective-permute-start | bytes 1769480 | tf_op jit(solution)/shard_map/ppermute | solution.py:123
  406.3 22.2 %attend_back.1 = (bf16[1,512,768]{2,1,0:T(8,128)(2,1)}, bf16[1,1024,768]{2,1,0:T(8,128)(2,1)}, bf16[1,1024,768]{2,1,0:T(8,128)(2,1)}) custom-call(bf16[1,512,768]{2,1,0:T(8,128)(2,1)} %fusion.83.query_ref, bf16[1,1024,768]{2,1,0:T(8,128)(2,1)} %fusion.76.keys_ref, bf16[1,1024,768]{2,1,0:T(8,128)(2,1)} %fusion.77.vals_ref, ...), custom_call_target="tpu_custom_call" | custom-call | flops 4026531840 | bytes 9437184 | tf_op jit(solution)/shard_map/attend_back/pallas_call | solution.py:98
  439.9 10.7 %collective-permute-start.23 = (bf16[256,768]{0,1:T(8,128)(2,1)}, bf16[256,768]{0,1:T(8,128)(2,1)}, u32[]{:S(2)}, u32[]{:S(2)}) collective-permute-start(bf16[256,768]{0,1:T(8,128)(2,1)} %get-tuple-element.71), channel_id=1, source_target_pairs={{0,8},{4,12},{8,0},{12,4},{16,24},{20,28},{24,16},{28,20},{1,9},{5... | collective-permute-start | bytes 1179656 | tf_op jit(solution)/shard_map/ppermute | solution.py:123
  478.6 30.3 %collective-permute-done.25 = bf16[256,768]{0,1:T(8,128)(2,1)S(1)} collective-permute-done((bf16[256,768]{0,1:T(8,128)(2,1)}, bf16[256,768]{0,1:T(8,128)(2,1)S(1)}, u32[]{:S(2)}, u32[]{:S(2)}) %collective-permute-start.25) | collective-permute-done | bytes 393248 | tf_op jit(solution)/shard_map/ppermute | solution.py:123
  510.2 7.9 collective-permute-done.26
  528.6 13.2 %collective-permute-start.58 = (bf16[96,384]{1,0:T(8,128)(2,1)S(1)}, bf16[96,384]{1,0:T(8,128)(2,1)S(1)}, u32[]{:S(2)}, u32[]{:S(2)}) collective-permute-start(bf16[96,384]{1,0:T(8,128)(2,1)S(1)} %get-tuple-element.106), channel_id=1, source_target_pairs={{0,8},{4,12},{8,0},{12,4},{16,24},{20,28},{24,16},{28,20},{1,9},{5... | collective-permute-start | bytes 221192 | tf_op jit(solution)/shard_map/ppermute | solution.py:123
  560.7 31.7 %collective-permute-done.64 = bf16[48,384]{1,0:T(8,128)(2,1)S(1)} collective-permute-done((bf16[48,384]{1,0:T(8,128)(2,1)S(1)}, bf16[48,384]{1,0:T(8,128)(2,1)S(1)}, u32[]{:S(2)}, u32[]{:S(2)}) %collective-permute-start.64) | collective-permute-done | bytes 36896 | tf_op jit(solution)/shard_map/ppermute | solution.py:123
  604.2 45.4 %all-reduce = (f32[768]{0:T(1024)}, f32[768]{0:T(1024)}, f32[768,8]{0,1:T(8,128)}) all-reduce(f32[768]{0:T(1024)S(1)} %get-tuple-element.45, f32[768]{0:T(1024)S(1)} %copy-done.81, f32[768,8]{0,1:T(8,128)S(1)} %copy-done.60), channel_id=1, replica_groups=mesh['expert'=8,'context'=2,'dp'=2] {'expert','context','dp'}, use_global_device_ids=true, to_apply=%region_26.27 | all-reduce | flops 7680 | bytes 61440 | tf_op jit(solution)/shard_map/psum | solution.py:301
  701.3 9.7 %collective-permute-start.73 = (bf16[768,384]{1,0:T(8,128)(2,1)}, bf16[768,384]{1,0:T(8,128)(2,1)S(1)}, u32[]{:S(2)}, u32[]{:S(2)}) collective-permute-start(bf16[768,384]{1,0:T(8,128)(2,1)} %constant_dynamic-update-slice_fusion.44), channel_id=1, source_target_pairs={{0,1},{1,0},{2,3},{3,2},{4,5},{5,4},{6,7},{7,6},{8,9},{9,8},{10,11... | collective-permute-start | bytes 1769480 | tf_op jit(solution)/shard_map/ppermute | solution.py:123
  746.0 6.8 collective-permute-start.54
  756.6 5.9 collective-permute-start.109
  795.7 8.0 copy.49
  (625 shorter events, 328.6 us)
Async XLA Ops:
  7.2 796.4 %reduce-scatter.3.cloned.1.call-start = ((), (), s32[]{:S(2)}) async-start(), calls=%async_computation.2 | async-start | bytes 5898240 | tf_op jit(solution)/shard_map/reduce_scatter | solution.py:305
  15.3 158.3 %collective-permute-start.14 = (bf16[256,768]{0,1:T(8,128)(2,1)}, bf16[256,768]{0,1:T(8,128)(2,1)}, u32[]{:S(2)}, u32[]{:S(2)}) collective-permute-start(bf16[256,768]{0,1:T(8,128)(2,1)} %get-tuple-element.78), channel_id=1, source_target_pairs={{0,16},{4,20},{8,24},{12,28},{16,0},{20,4},{24,8},{28,12},{1,17},{... | collective-permute-start | bytes 1179656 | tf_op jit(solution)/shard_map/ppermute | solution.py:123
  58.9 44.6 %collective-permute-start.1 = (bf16[256,768]{1,0:T(8,128)(2,1)S(1)}, bf16[256,768]{1,0:T(8,128)(2,1)S(1)}, u32[]{:S(2)}, u32[]{:S(2)}) collective-permute-start(bf16[256,768]{1,0:T(8,128)(2,1)S(1)} %get-tuple-element.97), channel_id=1, source_target_pairs={{0,16},{4,20},{8,24},{12,28},{16,0},{20,4},{24,8},{28,12},{1,17},{... | collective-permute-start | bytes 1179656 | tf_op jit(solution)/shard_map/ppermute | solution.py:123
  59.0 62.3 %collective-permute-start.2 = (bf16[256,768]{1,0:T(8,128)(2,1)S(1)}, bf16[256,768]{1,0:T(8,128)(2,1)S(1)}, u32[]{:S(2)}, u32[]{:S(2)}) collective-permute-start(bf16[256,768]{1,0:T(8,128)(2,1)S(1)} %get-tuple-element.96), channel_id=1, source_target_pairs={{0,20},{4,16},{8,28},{12,24},{16,4},{20,0},{24,12},{28,8},{1,21},{... | collective-permute-start | bytes 1179656 | tf_op jit(solution)/shard_map/ppermute | solution.py:123
  62.3 59.3 %collective-permute-start.3 = (bf16[256,768]{1,0:T(8,128)(2,1)S(1)}, bf16[256,768]{1,0:T(8,128)(2,1)S(1)}, u32[]{:S(2)}, u32[]{:S(2)}) collective-permute-start(bf16[256,768]{1,0:T(8,128)(2,1)S(1)} %get-tuple-element.95), channel_id=1, source_target_pairs={{0,24},{4,28},{8,16},{12,20},{16,8},{20,12},{24,0},{28,4},{1,25},{... | collective-permute-start | bytes 1179656 | tf_op jit(solution)/shard_map/ppermute | solution.py:123
  63.4 65.7 %collective-permute-start.4 = (bf16[256,768]{1,0:T(8,128)(2,1)S(1)}, bf16[256,768]{1,0:T(8,128)(2,1)S(1)}, u32[]{:S(2)}, u32[]{:S(2)}) collective-permute-start(bf16[256,768]{1,0:T(8,128)(2,1)S(1)} %get-tuple-element.94), channel_id=1, source_target_pairs={{0,28},{4,24},{8,20},{12,16},{16,12},{20,8},{24,4},{28,0},{1,29},{... | collective-permute-start | bytes 1179656 | tf_op jit(solution)/shard_map/ppermute | solution.py:123
  103.5 70.9 %collective-permute-start.15 = (bf16[256,768]{0,1:T(8,128)(2,1)S(1)}, bf16[256,768]{0,1:T(8,128)(2,1)S(1)}, u32[]{:S(2)}, u32[]{:S(2)}) collective-permute-start(bf16[256,768]{0,1:T(8,128)(2,1)S(1)} %copy-done.42), channel_id=1, source_target_pairs={{0,20},{4,16},{8,28},{12,24},{16,4},{20,0},{24,12},{28,8},{1,21},{... | collective-permute-start | bytes 1179656 | tf_op jit(solution)/shard_map/ppermute | solution.py:123
  129.1 43.6 %collective-permute-start.7 = (bf16[256,768]{1,0:T(8,128)(2,1)S(1)}, bf16[256,768]{1,0:T(8,128)(2,1)S(1)}, u32[]{:S(2)}, u32[]{:S(2)}) collective-permute-start(bf16[256,768]{1,0:T(8,128)(2,1)S(1)} %get-tuple-element.91), channel_id=1, source_target_pairs={{0,12},{4,8},{8,4},{12,0},{16,28},{20,24},{24,20},{28,16},{1,13},{... | collective-permute-start | bytes 1179656 | tf_op jit(solution)/shard_map/ppermute | solution.py:123
  172.7 41.8 %collective-permute-start.10 = (bf16[256,768]{0,1:T(8,128)(2,1)}, bf16[256,768]{0,1:T(8,128)(2,1)}, u32[]{:S(2)}, u32[]{:S(2)}) collective-permute-start(bf16[256,768]{0,1:T(8,128)(2,1)} %get-tuple-element.87), channel_id=1, source_target_pairs={{0,12},{4,8},{8,4},{12,0},{16,28},{20,24},{24,20},{28,16},{1,13},{... | collective-permute-start | bytes 1179656 | tf_op jit(solution)/shard_map/ppermute | solution.py:123
  173.6 40.9 %collective-permute-start.8 = (bf16[256,768]{0,1:T(8,128)(2,1)}, bf16[256,768]{0,1:T(8,128)(2,1)}, u32[]{:S(2)}, u32[]{:S(2)}) collective-permute-start(bf16[256,768]{0,1:T(8,128)(2,1)} %get-tuple-element.89), channel_id=1, source_target_pairs={{0,4},{4,0},{8,12},{12,8},{16,20},{20,16},{24,28},{28,24},{1,5},{5... | collective-permute-start | bytes 1179656 | tf_op jit(solution)/shard_map/ppermute | solution.py:123
  174.4 40.1 %collective-permute-start.9 = (bf16[256,768]{0,1:T(8,128)(2,1)}, bf16[256,768]{0,1:T(8,128)(2,1)}, u32[]{:S(2)}, u32[]{:S(2)}) collective-permute-start(bf16[256,768]{0,1:T(8,128)(2,1)} %get-tuple-element.88), channel_id=1, source_target_pairs={{0,8},{4,12},{8,0},{12,4},{16,24},{20,28},{24,16},{28,20},{1,9},{5... | collective-permute-start | bytes 1179656 | tf_op jit(solution)/shard_map/ppermute | solution.py:123
  242.5 564.1 %reduce-scatter.5.cloned.1.call-start = ((), (), s32[]{:S(2)}) async-start(), calls=%async_computation.3 | async-start | bytes 5898240 | tf_op jit(solution)/shard_map/reduce_scatter | solution.py:305
  255.6 67.9 %collective-permute-start.29 = (f32[2,128]{1,0:T(2,128)S(1)}, f32[2,128]{1,0:T(2,128)S(1)}, u32[]{:S(2)}, u32[]{:S(2)}) collective-permute-start(f32[2,128]{1,0:T(2,128)S(1)} %get-tuple-element.134), channel_id=1, source_target_pairs={{0,4},{4,0},{8,12},{12,8},{16,20},{20,16},{24,28},{28,24},{1,5},{5... | collective-permute-start | bytes 3080 | tf_op jit(solution)/shard_map/ppermute | solution.py:123
  256.4 69.2 %collective-permute-start.30 = (f32[2,128]{1,0:T(2,128)S(1)}, f32[2,128]{1,0:T(2,128)S(1)}, u32[]{:S(2)}, u32[]{:S(2)}) collective-permute-start(f32[2,128]{1,0:T(2,128)S(1)} %get-tuple-element.133), channel_id=1, source_target_pairs={{0,8},{4,12},{8,0},{12,4},{16,24},{20,28},{24,16},{28,20},{1,9},{5... | collective-permute-start | bytes 3080 | tf_op jit(solution)/shard_map/ppermute | solution.py:123
  266.1 61.9 %collective-permute-start.31 = (f32[2,128]{1,0:T(2,128)}, f32[2,128]{1,0:T(2,128)}, u32[]{:S(2)}, u32[]{:S(2)}) collective-permute-start(f32[2,128]{1,0:T(2,128)} %get-tuple-element.132), channel_id=1, source_target_pairs={{0,12},{4,8},{8,4},{12,0},{16,28},{20,24},{24,20},{28,16},{1,13},{... | collective-permute-start | bytes 3080 | tf_op jit(solution)/shard_map/ppermute | solution.py:123
  279.4 50.1 %collective-permute-start.32 = (f32[2,128]{1,0:T(2,128)}, f32[2,128]{1,0:T(2,128)}, u32[]{:S(2)}, u32[]{:S(2)}) collective-permute-start(f32[2,128]{1,0:T(2,128)} %get-tuple-element.131), channel_id=1, source_target_pairs={{0,16},{4,20},{8,24},{12,28},{16,0},{20,4},{24,8},{28,12},{1,17},{... | collective-permute-start | bytes 3080 | tf_op jit(solution)/shard_map/ppermute | solution.py:123
  283.3 47.4 %collective-permute-start.33 = (f32[2,128]{1,0:T(2,128)}, f32[2,128]{1,0:T(2,128)}, u32[]{:S(2)}, u32[]{:S(2)}) collective-permute-start(f32[2,128]{1,0:T(2,128)} %get-tuple-element.130), channel_id=1, source_target_pairs={{0,20},{4,16},{8,28},{12,24},{16,4},{20,0},{24,12},{28,8},{1,21},{... | collective-permute-start | bytes 3080 | tf_op jit(solution)/shard_map/ppermute | solution.py:123
  393.6 148.2 %collective-permute-start.92 = (bf16[768,384]{1,0:T(8,128)(2,1)}, bf16[768,384]{1,0:T(8,128)(2,1)}, u32[]{:S(2)}, u32[]{:S(2)}) collective-permute-start(bf16[768,384]{1,0:T(8,128)(2,1)} %constant_dynamic-slice_fusion.8), channel_id=1, source_target_pairs={{0,1},{1,0},{2,3},{3,2},{4,5},{5,4},{6,7},{7,6},{8,9},{9,8},{10,11... | collective-permute-start | bytes 1769480 | tf_op jit(solution)/shard_map/ppermute | solution.py:123
  463.9 45.1 %collective-permute-start.25 = (bf16[256,768]{0,1:T(8,128)(2,1)}, bf16[256,768]{0,1:T(8,128)(2,1)S(1)}, u32[]{:S(2)}, u32[]{:S(2)}) collective-permute-start(bf16[256,768]{0,1:T(8,128)(2,1)} %get-tuple-element.69), channel_id=1, source_target_pairs={{0,16},{4,20},{8,24},{12,28},{16,0},{20,4},{24,8},{28,12},{1,17},{... | collective-permute-start | bytes 1179656 | tf_op jit(solution)/shard_map/ppermute | solution.py:123
  468.4 49.8 %collective-permute-start.26 = (bf16[256,768]{0,1:T(8,128)(2,1)S(1)}, bf16[256,768]{0,1:T(8,128)(2,1)S(1)}, u32[]{:S(2)}, u32[]{:S(2)}) collective-permute-start(bf16[256,768]{0,1:T(8,128)(2,1)S(1)} %copy-done.48), channel_id=1, source_target_pairs={{0,20},{4,16},{8,28},{12,24},{16,4},{20,0},{24,12},{28,8},{1,21},{... | collective-permute-start | bytes 1179656 | tf_op jit(solution)/shard_map/ppermute | solution.py:123
  471.2 49.6 %collective-permute-start.27 = (bf16[256,768]{0,1:T(8,128)(2,1)S(1)}, bf16[256,768]{0,1:T(8,128)(2,1)S(1)}, u32[]{:S(2)}, u32[]{:S(2)}) collective-permute-start(bf16[256,768]{0,1:T(8,128)(2,1)S(1)} %copy-done.47), channel_id=1, source_target_pairs={{0,24},{4,28},{8,16},{12,20},{16,8},{20,12},{24,0},{28,4},{1,25},{... | collective-permute-start | bytes 1179656 | tf_op jit(solution)/shard_map/ppermute | solution.py:123
  474.6 47.0 %collective-permute-start.28 = (bf16[256,768]{0,1:T(8,128)(2,1)S(1)}, bf16[256,768]{0,1:T(8,128)(2,1)S(1)}, u32[]{:S(2)}, u32[]{:S(2)}) collective-permute-start(bf16[256,768]{0,1:T(8,128)(2,1)S(1)} %copy-done.46), channel_id=1, source_target_pairs={{0,28},{4,24},{8,20},{12,16},{16,12},{20,8},{24,4},{28,0},{1,29},{... | collective-permute-start | bytes 1179656 | tf_op jit(solution)/shard_map/ppermute | solution.py:123
  509.0 34.8 %collective-permute-start.38 = (bf16[768,384]{1,0:T(8,128)(2,1)S(1)}, bf16[768,384]{1,0:T(8,128)(2,1)S(1)}, u32[]{:S(2)}, u32[]{:S(2)}) collective-permute-start(bf16[768,384]{1,0:T(8,128)(2,1)S(1)} %constant_dynamic-slice_fusion.35), channel_id=1, source_target_pairs={{0,2},{2,0},{1,3},{3,1},{4,6},{6,4},{5,7},{7,5},{8,10},{10,8},{9,1... | collective-permute-start | bytes 1769480 | tf_op jit(solution)/shard_map/ppermute | solution.py:123
  520.8 39.2 %collective-permute-start.74 = (bf16[768,384]{1,0:T(8,128)(2,1)S(1)}, bf16[768,384]{1,0:T(8,128)(2,1)S(1)}, u32[]{:S(2)}, u32[]{:S(2)}) collective-permute-start(bf16[768,384]{1,0:T(8,128)(2,1)S(1)} %copy-done.34), channel_id=1, source_target_pairs={{0,1},{1,0},{2,3},{3,2},{4,5},{5,4},{6,7},{7,6},{8,9},{9,8},{10,11... | collective-permute-start | bytes 1769480 | tf_op jit(solution)/shard_map/ppermute | solution.py:123
  552.1 46.0 %collective-permute-start.36 = (bf16[1,512,768]{2,1,0:T(8,128)(2,1)S(1)}, bf16[1,512,768]{2,1,0:T(8,128)(2,1)S(1)}, u32[]{:S(2)}, u32[]{:S(2)}) collective-permute-start(bf16[1,512,768]{2,1,0:T(8,128)(2,1)S(1)} %slice.253), channel_id=1, source_target_pairs={{0,2},{2,0},{1,3},{3,1},{4,6},{6,4},{5,7},{7,5},{8,10},{10,8},{9,1... | collective-permute-start | bytes 2359304 | tf_op jit(solution)/shard_map/ppermute | solution.py:123
  557.3 41.1 %collective-permute-start.37 = (bf16[1,512,768]{2,1,0:T(8,128)(2,1)S(1)}, bf16[1,512,768]{2,1,0:T(8,128)(2,1)S(1)}, u32[]{:S(2)}, u32[]{:S(2)}) collective-permute-start(bf16[1,512,768]{2,1,0:T(8,128)(2,1)S(1)} %slice.255), channel_id=1, source_target_pairs={{0,2},{2,0},{1,3},{3,1},{4,6},{6,4},{5,7},{7,5},{8,10},{10,8},{9,1... | collective-permute-start | bytes 2359304 | tf_op jit(solution)/shard_map/ppermute | solution.py:123
  557.4 111.6 %collective-permute-start.93 = (bf16[384,384]{1,0:T(8,128)(2,1)}, bf16[384,384]{1,0:T(8,128)(2,1)}, u32[]{:S(2)}, u32[]{:S(2)}) collective-permute-start(bf16[384,384]{1,0:T(8,128)(2,1)} %constant_dynamic-slice_fusion.7), channel_id=1, source_target_pairs={{0,2},{2,0},{1,3},{3,1},{4,6},{6,4},{5,7},{7,5},{8,10},{10,8},{9,1... | collective-permute-start | bytes 884744 | tf_op jit(solution)/shard_map/ppermute | solution.py:123
  558.8 118.7 %collective-permute-start.39 = (bf16[384,384]{1,0:T(8,128)(2,1)}, bf16[384,384]{1,0:T(8,128)(2,1)}, u32[]{:S(2)}, u32[]{:S(2)}) collective-permute-start(bf16[384,384]{1,0:T(8,128)(2,1)} %constant_dynamic-slice_fusion.34), channel_id=1, source_target_pairs={{0,1},{1,0},{2,3},{3,2},{4,5},{5,4},{6,7},{7,6},{8,9},{9,8},{10,11... | collective-permute-start | bytes 884744 | tf_op jit(solution)/shard_map/ppermute | solution.py:123
  595.9 77.7 %collective-permute-start.75 = (bf16[384,384]{1,0:T(8,128)(2,1)}, bf16[384,384]{1,0:T(8,128)(2,1)}, u32[]{:S(2)}, u32[]{:S(2)}) collective-permute-start(bf16[384,384]{1,0:T(8,128)(2,1)} %constant_dynamic-slice_fusion.16), channel_id=1, source_target_pairs={{0,2},{2,0},{1,3},{3,1},{4,6},{6,4},{5,7},{7,5},{8,10},{10,8},{9,1... | collective-permute-start | bytes 884744 | tf_op jit(solution)/shard_map/ppermute | solution.py:123
  598.0 51.6 %collective-permute-start.66 = (bf16[96,384]{1,0:T(8,128)(2,1)S(1)}, bf16[96,384]{1,0:T(8,128)(2,1)S(1)}, u32[]{:S(2)}, u32[]{:S(2)}) collective-permute-start(bf16[96,384]{1,0:T(8,128)(2,1)S(1)} %constant_dynamic-update-slice_fusion.52), channel_id=1, source_target_pairs={{0,4},{4,0},{8,12},{12,8},{16,20},{20,16},{24,28},{28,24},{1,5},{5... | collective-permute-start | bytes 221192 | tf_op jit(solution)/shard_map/ppermute | solution.py:123
  598.4 52.8 %collective-permute-start.67 = (bf16[96,384]{1,0:T(8,128)(2,1)S(1)}, bf16[96,384]{1,0:T(8,128)(2,1)S(1)}, u32[]{:S(2)}, u32[]{:S(2)}) collective-permute-start(bf16[96,384]{1,0:T(8,128)(2,1)S(1)} %constant_dynamic-update-slice_fusion.52), channel_id=1, source_target_pairs={{0,8},{4,12},{8,0},{12,4},{16,24},{20,28},{24,16},{28,20},{1,9},{5... | collective-permute-start | bytes 221192 | tf_op jit(solution)/shard_map/ppermute | solution.py:123
  701.3 72.0 %collective-permute-start.73 = (bf16[768,384]{1,0:T(8,128)(2,1)}, bf16[768,384]{1,0:T(8,128)(2,1)S(1)}, u32[]{:S(2)}, u32[]{:S(2)}) collective-permute-start(bf16[768,384]{1,0:T(8,128)(2,1)} %constant_dynamic-update-slice_fusion.44), channel_id=1, source_target_pairs={{0,1},{1,0},{2,3},{3,2},{4,5},{5,4},{6,7},{7,6},{8,9},{9,8},{10,11... | collective-permute-start | bytes 1769480 | tf_op jit(solution)/shard_map/ppermute | solution.py:123
  (190 other events, 2687.9 us)
Sparse Core Ops, SparseCore 0:
  242.6 59.6 reduce-scatter.2
  328.1 52.6 reduce-scatter.4

commit v2 on v1

--- a/solution.py
+++ b/solution.py
@@ -127,55 +127,47 @@
     return [swap(block, axis, shift) for shift in range(lax.axis_size(axis))]
 
 
-def scatter_sum(block, axis):
-    size = block.shape[0] // lax.axis_size(axis)
-    me = lax.axis_index(axis)
-    total = None
-    for shift in range(lax.axis_size(axis)):
-        piece = lax.dynamic_slice_in_dim(block, (me ^ shift) * size, size, 0)
-        piece = swap(piece, axis, shift).astype(FULL)
-        total = piece if total is None else total + piece
-    return total.astype(LOW)
-
-
-def gather_in_order(block, axis):
-    size = block.shape[0]
-    me = lax.axis_index(axis)
-    out = jnp.zeros((size * lax.axis_size(axis),) + block.shape[1:], block.dtype)
-    for shift, piece in enumerate(gather_near_first(block, axis)):
-        out = lax.dynamic_update_slice_in_dim(out, piece, (me ^ shift) * size, 0)
-    return out
+def bits_of(axis):
+    size, bits = lax.axis_size(axis), []
+    while size > 1:
+        size //= 2
+        bits.append((axis, size))
+    return bits
+
+
+def halve(value, axis, bit):
+    size = value.shape[0] // 2
+    high = (lax.axis_index(axis) // bit) % 2
+    kept = lax.dynamic_slice_in_dim(value, high * size, size, 0)
+    given = lax.dynamic_slice_in_dim(value, (1 - high) * size, size, 0)
+    return (kept.astype(FULL) + swap(given, axis, bit).astype(FULL)).astype(LOW)
+
+
+def double(value, axis, bit):
+    high = (lax.axis_index(axis) // bit) % 2
+    other = swap(value, axis, bit)
+    return jnp.concatenate(
+        [jnp.where(high == 0, value, other), jnp.where(high == 0, other, value)], axis=0
+    )
 
 
 def sum_everywhere(part, order):
     high, wide = part.shape
-    value = part.astype(LOW).reshape(high, 2, wide // 2).transpose(1, 0, 2)
-    value = value.reshape(2 * high, wide // 2)
-    for axis in order:
-        value = scatter_sum(value, axis)
-    for axis in order[::-1]:
-        value = gather_in_order(value, axis)
-    return value.reshape(2, high, wide // 2).transpose(1, 0, 2).reshape(high, wide).astype(FULL)
-
-
-def expert_rows(arrived, up, w_router, weight_in, weight_back, mine):
-    gate_probs = jax.nn.softmax(
-        jnp.dot(arrived, w_router, preferred_element_type=FULL), axis=-1
-    )
-    column = (lax.broadcasted_iota(jnp.int32, gate_probs.shape, 1) == mine).astype(FULL)
-    gate = jnp.sum(gate_probs * column, axis=-1, keepdims=True)
-    hidden = jnp.dot(arrived, weight_in, preferred_element_type=FULL)
-    active, gelu_back = jax.vjp(jax.nn.gelu, hidden)
-    active_low = active.astype(LOW)
-    produced = jnp.dot(active_low, weight_back, preferred_element_type=FULL)
-    up_full = up.astype(FULL)
-    d_gate = jnp.sum(up_full * produced, axis=-1)
-    gated = (gate * produced).astype(LOW)
-    d_produced = (gate * up_full).astype(LOW)
-    d_active = contract(d_produced, weight_back, 1, 1)
-    d_hidden = gelu_back(d_active)[0].astype(LOW)
-    d_arrived = contract(d_hidden, weight_in, 1, 1).astype(LOW)
-    return active_low, d_produced, d_hidden, gated, d_gate, d_arrived
+    strip = 384
+    value = part.astype(LOW).reshape(high, wide // strip, strip).transpose(1, 0, 2)
+    value = value.reshape(-1, strip)
+    for axis, bit in order:
+        value = halve(value, axis, bit)
+    for axis, bit in order[::-1]:
+        value = double(value, axis, bit)
+    value = value.reshape(wide // strip, high, strip).transpose(1, 0, 2)
+    return value.reshape(high, wide).astype(FULL)
+
+
+def sum_small(value, order):
+    for axis, bit in order:
+        value = value + swap(value, axis, bit)
+    return value
 
 
 def body(tokens, gain_one, w_qkv, w_out, gain_two, w_router, w_in, w_back, expert_ids, cotangent):
@@ -190,35 +182,22 @@
     tokens_img = jnp.concatenate(gather_near_first(tokens, "context"), axis=1)
 
     routes = expert_ids.reshape(rows, TOPK).T
-    owners = mine ^ lax.broadcasted_iota(jnp.int32, (experts, 1), 0)
+    owners = lax.broadcasted_iota(jnp.int32, (experts, 1), 0)
     named = (routes[0][None] == owners) | (routes[1][None] == owners)
     place = jnp.where(named, jnp.cumsum(named.astype(jnp.int32), axis=1) - 1, -1)
-    choose = (
-        place[:, None, :] == lax.broadcasted_iota(jnp.int32, (experts, capacity, rows), 1)
-    ).astype(LOW)
-    far = experts // 2
-    groups = (range(far), range(far, experts))
-
-    def dispatch(values, group):
-        chosen = choose[group.start : group.stop].reshape(-1, rows)
-        sent = jnp.dot(chosen, values, preferred_element_type=FULL).astype(LOW)
-        return [
-            swap(sent[n * capacity : (n + 1) * capacity], "expert", shift)
-            for n, shift in enumerate(group)
-        ]
-
-    def send_back(values, group):
-        return [
-            swap(values[n * capacity : (n + 1) * capacity], "expert", shift)
-            for n, shift in enumerate(group)
-        ]
-
-    def collect(pieces):
-        return contract(choose.reshape(-1, rows), jnp.concatenate(pieces, axis=0), 0, 0)
+    taken = place[:, None, :] == lax.broadcasted_iota(jnp.int32, (experts, capacity, rows), 1)
+    choose = taken.astype(LOW).reshape(-1, rows)
+
+    def exchange(values):
+        return lax.all_to_all(
+            values.reshape(experts, capacity, width), "expert", 0, 0, tiled=True
+        ).reshape(-1, width)
+
+    def dispatch(values):
+        return exchange(jnp.dot(choose, values, preferred_element_type=FULL).astype(LOW))
 
     up_rows = cotangent.reshape(rows, width)
-    up_far = jnp.concatenate(dispatch(up_rows, groups[1]), axis=0)
-    up_near = jnp.concatenate(dispatch(up_rows, groups[0]), axis=0)
+    arrived_up = dispatch(up_rows)
 
     inputs = tokens.astype(FULL)
     normed, first_back = jax.vjp(layer_norm, inputs, gain_one)
@@ -239,36 +218,38 @@
     second, second_back = jax.vjp(layer_norm, resid, gain_two)
     second_rows = second.astype(LOW).reshape(rows, width)
 
-    arrived_far = jnp.concatenate(dispatch(second_rows, groups[1]), axis=0)
-    arrived_near = jnp.concatenate(dispatch(second_rows, groups[0]), axis=0)
-    act_n, dp_n, dh_n, gated_n, dg_n, da_n = expert_rows(
-        arrived_near, up_near, w_router, weight_in, weight_back, mine
-    )
-    act_f, dp_f, dh_f, gated_f, dg_f, da_f = expert_rows(
-        arrived_far, up_far, w_router, weight_in, weight_back, mine
-    )
-    d_rows_near = send_back(da_n, groups[0])
-    d_rows_far = send_back(da_f, groups[1])
-    d_gate_back = [
-        swap(piece, "expert", shift)
-        for shift, piece in enumerate(
-            jnp.concatenate([dg_n, dg_f]).reshape(experts, -1, 128)
-        )
-    ]
-    back_part = contract(act_n, dp_n, 0, 0) + contract(act_f, dp_f, 0, 0)
-    in_part = contract(arrived_near, dh_n, 0, 0) + contract(arrived_far, dh_f, 0, 0)
-
-    d_rows = collect(d_rows_near + d_rows_far)
-    gated_f, gated_n, d_rows = lax.optimization_barrier((gated_f, gated_n, d_rows))
-    added = collect(send_back(gated_n, groups[0]) + send_back(gated_f, groups[1]))
-    output = (resid + added.reshape(images, tok_ctx, width)).astype(LOW)
+    second_rows, arrived_up = lax.optimization_barrier((second_rows, arrived_up))
+    arrived = dispatch(second_rows)
+    hidden = jnp.dot(arrived, weight_in, preferred_element_type=FULL)
+    active_low = jax.nn.gelu(hidden).astype(LOW)
+    produced = jnp.dot(active_low, weight_back, preferred_element_type=FULL).astype(LOW)
+    returned = exchange(produced)
+    arrived_probs = jax.nn.softmax(
+        jnp.dot(arrived, w_router, preferred_element_type=FULL), axis=-1
+    )
+    column = (lax.broadcasted_iota(jnp.int32, arrived_probs.shape, 1) == mine).astype(FULL)
+    arrived_gate = jnp.sum(arrived_probs * column, axis=-1, keepdims=True)
+    d_produced = (arrived_gate * arrived_up.astype(FULL)).astype(LOW)
+    d_active = contract(d_produced, weight_back, 1, 1)
+    _, gelu_back = jax.vjp(jax.nn.gelu, hidden)
+    d_hidden = gelu_back(d_active)[0].astype(LOW)
+    d_arrived = contract(d_hidden, weight_in, 1, 1).astype(LOW)
+    d_arrived, returned, active_low, d_produced, arrived, d_hidden = lax.optimization_barrier(
+        (d_arrived, returned, active_low, d_produced, arrived, d_hidden)
+    )
+    returned_grad = exchange(d_arrived)
+    back_part = contract(active_low, d_produced, 0, 0)
+    in_part = contract(arrived, d_hidden, 0, 0)
+
     gate_probs = jax.nn.softmax(
         jnp.dot(second_rows, w_router, preferred_element_type=FULL), axis=-1
     )
-    d_gate_slots = jnp.stack(d_gate_back).reshape(experts, capacity)
-    d_gate_tok = jnp.sum(choose.astype(FULL) * d_gate_slots[:, :, None], axis=1)
-    to_column = (owners == lax.broadcasted_iota(jnp.int32, (experts, experts), 1)).astype(FULL)
-    d_probs = jnp.sum(d_gate_tok[:, :, None] * to_column[:, None, :], axis=0)
+    weighted = jnp.where(taken, gate_probs.T[:, None, :], 0.0).astype(LOW).reshape(-1, rows)
+    added = contract(weighted, returned, 0, 0)
+    output = (resid + added.reshape(images, tok_ctx, width)).astype(LOW)
+    met = contract(returned, up_rows, 1, 1).reshape(experts, capacity, rows)
+    d_probs = jnp.sum(jnp.where(taken, met, 0.0), axis=1).T
+    d_rows = contract(choose, returned_grad, 0, 0)
     d_logits = gate_probs * (d_probs - jnp.sum(gate_probs * d_probs, axis=-1, keepdims=True))
     d_logits_low = d_logits.astype(LOW)
     router_part = contract(second_rows, d_logits_low, 0, 0)
@@ -290,17 +271,26 @@
 
     d_keys = sum_context(d_keys_img)
     d_vals = sum_context(d_vals_img)
-    grad_out = sum_everywhere(grad_of(mixed_low, d_attn), ("dp", "context", "expert"))
-    grad_v = sum_everywhere(grad_of(normed_img, d_vals_img), ("dp", "context", "expert"))
-    grad_k = sum_everywhere(grad_of(normed_img, d_keys_img), ("dp", "expert", "context"))
-    grad_q = sum_everywhere(grad_of(normed_low, d_query), ("context", "dp", "expert"))
+    bits_e, bits_c, bits_d = bits_of("expert"), bits_of("context"), bits_of("dp")
+    plain = bits_d + bits_c + bits_e[::-1]
+    turned = bits_d + bits_e[::-1][:1] + bits_c + bits_e[::-1][1:]
+    grad_out = sum_everywhere(grad_of(mixed_low, d_attn), plain)
+    grad_v = sum_everywhere(grad_of(normed_img, d_vals_img), plain)
+    grad_qk = sum_everywhere(
+        jnp.concatenate(
+            [grad_of(normed_low, d_query), grad_of(normed_img, d_keys_img)], axis=-1
+        ),
+        turned,
+    )
     d_packed = jnp.concatenate([d_query, d_keys, d_vals], axis=-1)
     d_normed = jnp.einsum("ise,de->isd", d_packed, w_qkv, preferred_element_type=FULL)
     d_inputs_norm, gain_one_part = first_back(d_normed)
     grad_tokens = d_resid + d_inputs_norm
-    grad_router, grad_gain_one, grad_gain_two = lax.psum(
-        (router_part, gain_one_part, gain_two_part), EVERY
-    )
+    small = jnp.concatenate([router_part.reshape(-1), gain_one_part, gain_two_part])
+    small = sum_small(small.reshape(-1, 128), plain).reshape(-1)
+    grad_router = small[: -2 * width].reshape(width, experts)
+    grad_gain_one = small[-2 * width : -width]
+    grad_gain_two = small[-width:]
     grad_in, grad_back = (
         lax.psum_scatter(
             part[None].astype(LOW), ("context", "dp"), scatter_dimension=1, tiled=True
@@ -311,7 +301,7 @@
         output,
         grad_tokens,
         grad_gain_one,
-        jnp.concatenate([grad_q, grad_k, grad_v], axis=-1),
+        jnp.concatenate([grad_qk, grad_v], axis=-1),
         grad_out,
         grad_gain_two,
         grad_router,

time: 826 us -> 602 us (0.73)
  starting transfers between devices: 216 us -> 72.3 us
  local copies, waits for them, and re-layouts: 108 us -> 32.2 us
  waiting for transfers between devices: 183 us -> 240 us
  blocking collectives: 45.4 us -> 0 us
  matrix products: 178 us -> 168 us
    ppermute x110 -> x38, starting transfers between devices: 216 us -> 49.2 us  [swap(): return lax.ppermute(block, axis, partners(axis, shift)) if shift else block]
    all_to_all x0 -> x4, waiting for transfers between devices: none -> 158 us  [exchange(): lax.all_to_all(values.reshape(experts, capacity, width), 'expert', 0, 0,...]
    ppermute x110 -> x38, waiting for transfers between devices: 183 us -> 82.1 us  [swap(): return lax.ppermute(block, axis, partners(axis, shift)) if shift else block]
    psum x1 -> x0, blocking collectives: 45.4 us -> none  [body(): lax.psum((router_part, gain_one_part, gain_two_part), EVERY)]
    unnamed x239 -> x116, local copies, waits for them, and re-layouts: 37.4 us -> 8.44 us
    all_to_all x0 -> x4, starting transfers between devices: none -> 22.6 us  [exchange(): lax.all_to_all(values.reshape(experts, capacity, width), 'expert', 0, 0,...]
    dynamic_update_slice x44 -> x0, local copies, waits for them, and re-layouts: 21.2 us -> none  [gather_in_order(): out = lax.dynamic_update_slice_in_dim(out, piece, (me ^ shift) * size, 0)]
    dot_general x12 -> x9, matrix products: 101 us -> 91.7 us  [contract(): lax.dot_general(left, right, (((left_dim,), (right_dim,)), ((), ())), pre...]
  transfers between devices with their start and end apart: 112 -> 44, of which waited for: 17 -> 21; matrix products, arithmetic and copies ran while one was open for 34% -> 26% of each run, Pallas kernels for 4% -> 6%
where the time goes in v2:
time: 602 us; the launch traced here: 598 us
  waiting for transfers between devices  240 us (40%)
  matrix products  168 us (28%)
  starting transfers between devices  72.3 us (12%)
  Pallas kernels  35.8 us (6%)
  other arithmetic  33.7 us (6%)
  local copies, waits for them, and re-layouts  32.2 us (5%)
  between operations  15.9 us (3%)
    all_to_all x4, waiting for transfers between devices, exchange(): lax.all_to_all(values.reshape(experts, capacity, width), 'expert', 0, 0,...  158 us
    dot_general x9, matrix products, contract(): lax.dot_general(left, right, (((left_dim,), (right_dim,)), ((), ())), pre...  91.7 us
    ppermute x38, waiting for transfers between devices, swap(): return lax.ppermute(block, axis, partners(axis, shift)) if shift else block  82.1 us
    ppermute x38, starting transfers between devices, swap(): return lax.ppermute(block, axis, partners(axis, shift)) if shift else block  49.2 us
    dot_general x1, matrix products, body(): hidden = jnp.dot(arrived, weight_in, preferred_element_type=FULL)  23.9 us
    all_to_all x4, starting transfers between devices, exchange(): lax.all_to_all(values.reshape(experts, capacity, width), 'expert', 0, 0,...  22.6 us
    pallas_call x1, Pallas kernels, attend_back(): pl.pallas_call(attend_back_kernel, grid=(images, pairs), in_specs=[near,...  21.8 us
    dot_general x1, matrix products, body(): jnp.dot(active_low, weight_back, preferred_element_type=FULL).astype(LOW)  14.1 us
  transfers between devices with their start and end apart: 44, of which 21 were waited for; matrix products, arithmetic and copies ran while one was open for 26% of the time, Pallas kernels for 6%

profile of v2, /device:TPU:1, one launch (start us, length us, event | category | flops | bytes accessed | tf_op | source)
XLA Modules:
  0.0 598.3 jit_solution(5135473581195640476)
XLA Ops:
  10.1 4.6 convolution_convert_fusion.3
  14.7 7.1 %all-to-all-start = ((bf16[8,256,768]{2,1,0:T(8,128)(2,1)}), bf16[8,256,768]{2,1,0:T(8,128)(2,1)}, u32[]{:S(2)}, u32[]{:S(2)}) async-start(bf16[8,256,768]{2,1,0:T(8,128)(2,1)} %bitcast.232), calls=%async_computation | async-start | bytes 6291456 | tf_op jit(solution)/shard_map/all_to_all | solution.py:192
  28.8 11.3 %collective-permute-done = bf16[1,512,768]{2,1,0:T(8,128)(2,1)S(1)} collective-permute-done((bf16[1,512,768]{2,1,0:T(8,128)(2,1)S(1)}, bf16[1,512,768]{2,1,0:T(8,128)(2,1)S(1)}, u32[]{:S(2)}, u32[]{:S(2)}) %collective-permute-start) | collective-permute-done | bytes 786464 | tf_op jit(solution)/shard_map/ppermute | solution.py:123
  46.4 14.0 %attend.1 = (bf16[1,512,768]{2,1,0:T(8,128)(2,1)}, f32[1,6,2,512]{3,2,1,0:T(2,128)}) custom-call(bf16[1,512,768]{2,1,0:T(8,128)(2,1)} %fusion.60.query_ref, bf16[1,1024,768]{2,1,0:T(8,128)(2,1)} %fusion.58.keys_ref, bf16[1,1024,768]{2,1,0:T(8,128)(2,1)} %fusion.59.vals_ref), custom_call_target="tpu_custom_call" | custom-call | flops 1610612736 | bytes 4718592 | tf_op jit(solution)/shard_map/attend/pallas_call | solution.py:54
  64.4 27.2 %all-to-all-done = bf16[8,256,768]{2,1,0:T(8,128)(2,1)} async-done(((bf16[8,256,768]{2,1,0:T(8,128)(2,1)}), bf16[8,256,768]{2,1,0:T(8,128)(2,1)}, u32[]{:S(2)}, u32[]{:S(2)}) %all-to-all-start) | async-done | bytes 3145760 | tf_op jit(solution)/shard_map/all_to_all | solution.py:192
  95.1 5.0 all-to-all-start.1
  100.2 69.3 %all-to-all-done.1 = bf16[8,256,768]{2,1,0:T(8,128)(2,1)} async-done(((bf16[8,256,768]{2,1,0:T(8,128)(2,1)}), bf16[8,256,768]{2,1,0:T(8,128)(2,1)}, u32[]{:S(2)}, u32[]{:S(2)}) %all-to-all-start.1) | async-done | bytes 3145760 | tf_op jit(solution)/shard_map/all_to_all | solution.py:192
  172.5 23.9 %multiply_convert_fusion = (bf16[2048,3072]{1,0:T(8,128)(2,1)}, f32[2048,3072]{1,0:T(8,128)}) fusion(bf16[2048,768]{1,0:T(8,128)(2,1)} %bitcast.25, bf16[1,768,3072]{2,1,0:T(8,128)(2,1)} %param.16), kind=kOutput, calls=%fused_computation.9 | convolution fusion | flops 9720299520 | bytes 45613056 | tf_op jit(solution)/shard_map/dot_general | solution.py:223
  196.5 14.1 %fusion.20 = bf16[2048,768]{1,0:T(8,128)(2,1)} fusion(bf16[2048,3072]{1,0:T(8,128)(2,1)} %get-tuple-element.33, bf16[1,3072,768]{2,1,0:T(8,128)(2,1)S(1)} %bitcast.254), kind=kOutput, calls=%fused_computation.31 | convolution fusion | flops 9665249280 | bytes 20447232 | tf_op jit(solution)/shard_map/dot_general | solution.py:225
  210.5 5.2 all-to-all-start.2
  218.5 28.6 %fusion.6 = bf16[2048,3072]{1,0:T(8,128)(2,1)} fusion(f32[2048,3072]{1,0:T(8,128)} %get-tuple-element.91, bf16[2048,768]{1,0:T(8,128)(2,1)S(1)} %multiply_convert_fusion.1, bf16[1,3072,768]{2,1,0:T(8,128)(2,1)} %param.17), kind=kOutput, calls=%fused_computation.8 | convolution fusion | flops 9789505536 | bytes 45613056 | tf_op jit(solution)/shard_map/dot_general | solution.py:29
  247.1 14.2 %fusion.23 = bf16[2048,768]{1,0:T(8,128)(2,1)} fusion(bf16[2048,3072]{1,0:T(8,128)(2,1)} %fusion.6, bf16[1,768,3072]{2,1,0:T(8,128)(2,1)S(1)} %bitcast.256), kind=kOutput, calls=%fused_computation.32 | convolution fusion | flops 9665249280 | bytes 20447232 | tf_op jit(solution)/shard_map/dot_general | solution.py:29
  261.3 23.9 %all-to-all-done.2 = bf16[8,256,768]{2,1,0:T(8,128)(2,1)} async-done(((bf16[8,256,768]{2,1,0:T(8,128)(2,1)}), bf16[8,256,768]{2,1,0:T(8,128)(2,1)}, u32[]{:S(2)}, u32[]{:S(2)}) %all-to-all-start.2) | async-done | bytes 3145760 | tf_op jit(solution)/shard_map/all_to_all | solution.py:192
  285.2 15.3 %fusion.17 = bf16[1,768,3072]{2,1,0:T(8,128)(2,1)} fusion(bf16[2048,768]{1,0:T(8,128)(2,1)} %bitcast.25, bf16[2048,3072]{1,0:T(8,128)(2,1)} %fusion.6), kind=kOutput, calls=%fused_computation.21 | convolution fusion | flops 9666035712 | bytes 20447232 | tf_op jit(solution)/shard_map/dot_general | solution.py:29
  300.5 5.2 all-to-all-start.3
  308.4 4.6 select_reduce_fusion
  314.3 15.6 %fusion.18 = bf16[1,3072,768]{2,1,0:T(8,128)(2,1)} fusion(bf16[2048,3072]{1,0:T(8,128)(2,1)} %get-tuple-element.33, bf16[2048,768]{1,0:T(8,128)(2,1)} %copy-done.10), kind=kOutput, calls=%fused_computation.22 | convolution fusion | flops 9666035712 | bytes 20447232 | tf_op jit(solution)/shard_map/dot_general | solution.py:29
  332.3 5.2 fusion.51
  337.6 37.6 %all-to-all-done.3 = bf16[8,256,768]{2,1,0:T(8,128)(2,1)} async-done(((bf16[8,256,768]{2,1,0:T(8,128)(2,1)}), bf16[8,256,768]{2,1,0:T(8,128)(2,1)}, u32[]{:S(2)}, u32[]{:S(2)}) %all-to-all-start.3) | async-done | bytes 3145760 | tf_op jit(solution)/shard_map/all_to_all | solution.py:192
  375.2 5.3 fusion.49
  386.5 21.8 %attend_back.1 = (bf16[1,512,768]{2,1,0:T(8,128)(2,1)}, bf16[1,1024,768]{2,1,0:T(8,128)(2,1)}, bf16[1,1024,768]{2,1,0:T(8,128)(2,1)}) custom-call(bf16[1,512,768]{2,1,0:T(8,128)(2,1)} %fusion.60.query_ref, bf16[1,1024,768]{2,1,0:T(8,128)(2,1)} %fusion.58.keys_ref, bf16[1,1024,768]{2,1,0:T(8,128)(2,1)} %fusion.59.vals_ref, ...), custom_call_target="tpu_custom_call" | custom-call | flops 4026531840 | bytes 9437184 | tf_op jit(solution)/shard_map/attend_back/pallas_call | solution.py:98
  408.4 4.3 fusion.55
  422.9 4.4 fusion.52
  441.5 11.1 %collective-permute-done.1 = bf16[1,512,768]{2,1,0:T(8,128)(2,1)S(1)} collective-permute-done((bf16[1,512,768]{2,1,0:T(8,128)(2,1)}, bf16[1,512,768]{2,1,0:T(8,128)(2,1)S(1)}, u32[]{:S(2)}, u32[]{:S(2)}) %collective-permute-start.1) | collective-permute-done | bytes 786464 | tf_op jit(solution)/shard_map/ppermute | solution.py:123
  452.8 16.7 %collective-permute-done.2 = bf16[1,512,768]{2,1,0:T(8,128)(2,1)S(1)} collective-permute-done((bf16[1,512,768]{2,1,0:T(8,128)(2,1)S(1)}, bf16[1,512,768]{2,1,0:T(8,128)(2,1)S(1)}, u32[]{:S(2)}, u32[]{:S(2)}) %collective-permute-start.2) | collective-permute-done | bytes 786464 | tf_op jit(solution)/shard_map/ppermute | solution.py:123
  477.1 7.3 %collective-permute-done.4 = f32[60,128]{1,0:T(8,128)S(1)} collective-permute-done((f32[60,128]{1,0:T(8,128)S(1)}, f32[60,128]{1,0:T(8,128)S(1)}, u32[]{:S(2)}, u32[]{:S(2)}) %collective-permute-start.4) | collective-permute-done | bytes 30752 | tf_op jit(solution)/shard_map/ppermute | solution.py:123
  507.6 4.9 collective-permute-done.9
  514.1 4.3 collective-permute-done.10
  518.7 4.1 collective-permute-done.11
  523.1 4.6 collective-permute-done.12
  544.3 11.7 %collective-permute-start.37 = (bf16[768,384]{1,0:T(8,128)(2,1)}, bf16[768,384]{1,0:T(8,128)(2,1)}, u32[]{:S(2)}, u32[]{:S(2)}) collective-permute-start(bf16[768,384]{1,0:T(8,128)(2,1)} %pad_maximum_fusion.8), channel_id=1, source_target_pairs={{0,1},{1,0},{2,3},{3,2},{4,5},{5,4},{6,7},{7,6},{8,9},{9,8},{10,11... | collective-permute-start | bytes 1769480 | tf_op jit(solution)/shard_map/ppermute | solution.py:123
  559.6 6.0 collective-permute-start.17
  (326 shorter events, 143.8 us)
Async XLA Ops:
  14.7 77.0 %all-to-all-start = ((bf16[8,256,768]{2,1,0:T(8,128)(2,1)}), bf16[8,256,768]{2,1,0:T(8,128)(2,1)}, u32[]{:S(2)}, u32[]{:S(2)}) async-start(bf16[8,256,768]{2,1,0:T(8,128)(2,1)} %bitcast.232), calls=%async_computation | async-start | bytes 6291456 | tf_op jit(solution)/shard_map/all_to_all | solution.py:192
  21.8 18.3 %collective-permute-start = (bf16[1,512,768]{2,1,0:T(8,128)(2,1)S(1)}, bf16[1,512,768]{2,1,0:T(8,128)(2,1)S(1)}, u32[]{:S(2)}, u32[]{:S(2)}) collective-permute-start(bf16[1,512,768]{2,1,0:T(8,128)(2,1)S(1)} %copy-done.1), channel_id=1, source_target_pairs={{0,2},{2,0},{1,3},{3,1},{4,6},{6,4},{5,7},{7,5},{8,10},{10,8},{9,1... | collective-permute-start | bytes 2359304 | tf_op jit(solution)/shard_map/ppermute | solution.py:123
  95.1 74.4 %all-to-all-start.1 = ((bf16[8,256,768]{2,1,0:T(8,128)(2,1)}), bf16[8,256,768]{2,1,0:T(8,128)(2,1)}, u32[]{:S(2)}, u32[]{:S(2)}) async-start(bf16[8,256,768]{2,1,0:T(8,128)(2,1)} %bitcast.234), calls=%async_computation.1 | async-start | bytes 6291456 | tf_op jit(solution)/shard_map/all_to_all | solution.py:192
  210.5 74.6 %all-to-all-start.2 = ((bf16[8,256,768]{2,1,0:T(8,128)(2,1)}), bf16[8,256,768]{2,1,0:T(8,128)(2,1)}, u32[]{:S(2)}, u32[]{:S(2)}) async-start(bf16[8,256,768]{2,1,0:T(8,128)(2,1)} %bitcast.233), calls=%async_computation.2 | async-start | bytes 6291456 | tf_op jit(solution)/shard_map/all_to_all | solution.py:192
  215.8 361.8 %reduce-scatter.3.cloned.1.call-start = ((), (), s32[]{:S(2)}) async-start(), calls=%async_computation.6 | async-start | bytes 5898240 | tf_op jit(solution)/shard_map/reduce_scatter | solution.py:295
  300.5 74.7 %all-to-all-start.3 = ((bf16[8,256,768]{2,1,0:T(8,128)(2,1)}), bf16[8,256,768]{2,1,0:T(8,128)(2,1)}, u32[]{:S(2)}, u32[]{:S(2)}) async-start(bf16[8,256,768]{2,1,0:T(8,128)(2,1)} %bitcast.231), calls=%async_computation.3 | async-start | bytes 6291456 | tf_op jit(solution)/shard_map/all_to_all | solution.py:192
  305.8 274.7 %reduce-scatter.5.cloned.1.call-start = ((), (), s32[]{:S(2)}) async-start(), calls=%async_computation.7 | async-start | bytes 5898240 | tf_op jit(solution)/shard_map/reduce_scatter | solution.py:295
  418.0 20.7 %collective-permute-start.28 = (bf16[768,384]{1,0:T(8,128)(2,1)}, bf16[768,384]{1,0:T(8,128)(2,1)}, u32[]{:S(2)}, u32[]{:S(2)}) collective-permute-start(bf16[768,384]{1,0:T(8,128)(2,1)} %constant_dynamic-slice_fusion.4), channel_id=1, source_target_pairs={{0,1},{1,0},{2,3},{3,2},{4,5},{5,4},{6,7},{7,6},{8,9},{9,8},{10,11... | collective-permute-start | bytes 1769480 | tf_op jit(solution)/shard_map/ppermute | solution.py:123
  433.5 7.8 %collective-permute-start.18 = (bf16[768,384]{1,0:T(8,128)(2,1)S(1)}, bf16[768,384]{1,0:T(8,128)(2,1)S(1)}, u32[]{:S(2)}, u32[]{:S(2)}) collective-permute-start(bf16[768,384]{1,0:T(8,128)(2,1)S(1)} %constant_dynamic-slice_fusion.9), channel_id=1, source_target_pairs={{0,1},{1,0},{2,3},{3,2},{4,5},{5,4},{6,7},{7,6},{8,9},{9,8},{10,11... | collective-permute-start | bytes 1769480 | tf_op jit(solution)/shard_map/ppermute | solution.py:123
  433.6 19.0 %collective-permute-start.1 = (bf16[1,512,768]{2,1,0:T(8,128)(2,1)}, bf16[1,512,768]{2,1,0:T(8,128)(2,1)S(1)}, u32[]{:S(2)}, u32[]{:S(2)}) collective-permute-start(bf16[1,512,768]{2,1,0:T(8,128)(2,1)} %slice.57), channel_id=1, source_target_pairs={{0,2},{2,0},{1,3},{3,1},{4,6},{6,4},{5,7},{7,5},{8,10},{10,8},{9,1... | collective-permute-start | bytes 2359304 | tf_op jit(solution)/shard_map/ppermute | solution.py:123
  437.5 64.3 %collective-permute-start.8 = (bf16[1536,384]{1,0:T(8,128)(2,1)S(1)}, bf16[1536,384]{1,0:T(8,128)(2,1)S(1)}, u32[]{:S(2)}, u32[]{:S(2)}) collective-permute-start(bf16[1536,384]{1,0:T(8,128)(2,1)S(1)} %constant_dynamic-slice_fusion.14), channel_id=1, source_target_pairs={{0,1},{1,0},{2,3},{3,2},{4,5},{5,4},{6,7},{7,6},{8,9},{9,8},{10,11... | collective-permute-start | bytes 3538952 | tf_op jit(solution)/shard_map/ppermute | solution.py:123
  438.5 31.0 %collective-permute-start.2 = (bf16[1,512,768]{2,1,0:T(8,128)(2,1)S(1)}, bf16[1,512,768]{2,1,0:T(8,128)(2,1)S(1)}, u32[]{:S(2)}, u32[]{:S(2)}) collective-permute-start(bf16[1,512,768]{2,1,0:T(8,128)(2,1)S(1)} %copy-done.19), channel_id=1, source_target_pairs={{0,2},{2,0},{1,3},{3,1},{4,6},{6,4},{5,7},{7,5},{8,10},{10,8},{9,1... | collective-permute-start | bytes 2359304 | tf_op jit(solution)/shard_map/ppermute | solution.py:123
  440.1 47.5 %collective-permute-start.29 = (bf16[384,384]{1,0:T(8,128)(2,1)S(1)}, bf16[384,384]{1,0:T(8,128)(2,1)S(1)}, u32[]{:S(2)}, u32[]{:S(2)}) collective-permute-start(bf16[384,384]{1,0:T(8,128)(2,1)S(1)} %constant_dynamic-slice_fusion.3), channel_id=1, source_target_pairs={{0,2},{2,0},{1,3},{3,1},{4,6},{6,4},{5,7},{7,5},{8,10},{10,8},{9,1... | collective-permute-start | bytes 884744 | tf_op jit(solution)/shard_map/ppermute | solution.py:123
  475.0 13.6 %collective-permute-start.19 = (bf16[384,384]{1,0:T(8,128)(2,1)S(1)}, bf16[384,384]{1,0:T(8,128)(2,1)S(1)}, u32[]{:S(2)}, u32[]{:S(2)}) collective-permute-start(bf16[384,384]{1,0:T(8,128)(2,1)S(1)} %constant_dynamic-slice_fusion.8), channel_id=1, source_target_pairs={{0,2},{2,0},{1,3},{3,1},{4,6},{6,4},{5,7},{7,5},{8,10},{10,8},{9,1... | collective-permute-start | bytes 884744 | tf_op jit(solution)/shard_map/ppermute | solution.py:123
  476.3 8.1 %collective-permute-start.4 = (f32[60,128]{1,0:T(8,128)S(1)}, f32[60,128]{1,0:T(8,128)S(1)}, u32[]{:S(2)}, u32[]{:S(2)}) collective-permute-start(f32[60,128]{1,0:T(8,128)S(1)} %fusion.86), channel_id=1, source_target_pairs={{0,2},{2,0},{1,3},{3,1},{4,6},{6,4},{5,7},{7,5},{8,10},{10,8},{9,1... | collective-permute-start | bytes 92168 | tf_op jit(solution)/shard_map/ppermute | solution.py:123
  487.8 6.4 %collective-permute-start.30 = (bf16[192,384]{1,0:T(8,128)(2,1)S(1)}, bf16[192,384]{1,0:T(8,128)(2,1)S(1)}, u32[]{:S(2)}, u32[]{:S(2)}) collective-permute-start(bf16[192,384]{1,0:T(8,128)(2,1)S(1)} %constant_dynamic-slice_fusion.2), channel_id=1, source_target_pairs={{0,4},{4,0},{8,12},{12,8},{16,20},{20,16},{24,28},{28,24},{1,5},{5... | collective-permute-start | bytes 442376 | tf_op jit(solution)/shard_map/ppermute | solution.py:123
  502.2 10.3 %collective-permute-start.9 = (bf16[768,384]{1,0:T(8,128)(2,1)S(1)}, bf16[768,384]{1,0:T(8,128)(2,1)S(1)}, u32[]{:S(2)}, u32[]{:S(2)}) collective-permute-start(bf16[768,384]{1,0:T(8,128)(2,1)S(1)} %constant_dynamic-slice_fusion.13), channel_id=1, source_target_pairs={{0,4},{4,0},{8,12},{12,8},{16,20},{20,16},{24,28},{28,24},{1,5},{5... | collective-permute-start | bytes 1769480 | tf_op jit(solution)/shard_map/ppermute | solution.py:123
  502.5 5.0 collective-permute-start.33
  503.6 10.4 %collective-permute-start.23 = (bf16[48,384]{1,0:T(8,128)(2,1)S(1)}, bf16[48,384]{1,0:T(8,128)(2,1)S(1)}, u32[]{:S(2)}, u32[]{:S(2)}) collective-permute-start(bf16[48,384]{1,0:T(8,128)(2,1)S(1)} %add_convert_fusion.16), channel_id=1, source_target_pairs={{0,16},{4,20},{8,24},{12,28},{16,0},{20,4},{24,8},{28,12},{1,17},{... | collective-permute-start | bytes 110600 | tf_op jit(solution)/shard_map/ppermute | solution.py:123
  507.5 11.1 %collective-permute-start.34 = (bf16[96,384]{1,0:T(8,128)(2,1)S(1)}, bf16[96,384]{1,0:T(8,128)(2,1)S(1)}, u32[]{:S(2)}, u32[]{:S(2)}) collective-permute-start(bf16[96,384]{1,0:T(8,128)(2,1)S(1)} %pad_maximum_fusion.16), channel_id=1, source_target_pairs={{0,8},{4,12},{8,0},{12,4},{16,24},{20,28},{24,16},{28,20},{1,9},{5... | collective-permute-start | bytes 221192 | tf_op jit(solution)/shard_map/ppermute | solution.py:123
  512.7 5.6 collective-permute-start.10
  514.0 9.0 %collective-permute-start.24 = (bf16[96,384]{1,0:T(8,128)(2,1)S(1)}, bf16[96,384]{1,0:T(8,128)(2,1)S(1)}, u32[]{:S(2)}, u32[]{:S(2)}) collective-permute-start(bf16[96,384]{1,0:T(8,128)(2,1)S(1)} %pad_maximum_fusion.15), channel_id=1, source_target_pairs={{0,8},{4,12},{8,0},{12,4},{16,24},{20,28},{24,16},{28,20},{1,9},{5... | collective-permute-start | bytes 221192 | tf_op jit(solution)/shard_map/ppermute | solution.py:123
  518.6 13.3 %collective-permute-start.35 = (bf16[192,384]{1,0:T(8,128)(2,1)S(1)}, bf16[192,384]{1,0:T(8,128)(2,1)S(1)}, u32[]{:S(2)}, u32[]{:S(2)}) collective-permute-start(bf16[192,384]{1,0:T(8,128)(2,1)S(1)} %pad_maximum_fusion.14), channel_id=1, source_target_pairs={{0,4},{4,0},{8,12},{12,8},{16,20},{20,16},{24,28},{28,24},{1,5},{5... | collective-permute-start | bytes 442376 | tf_op jit(solution)/shard_map/ppermute | solution.py:123
  527.7 10.8 %collective-permute-start.25 = (bf16[192,384]{1,0:T(8,128)(2,1)S(1)}, bf16[192,384]{1,0:T(8,128)(2,1)S(1)}, u32[]{:S(2)}, u32[]{:S(2)}) collective-permute-start(bf16[192,384]{1,0:T(8,128)(2,1)S(1)} %pad_maximum_fusion.13), channel_id=1, source_target_pairs={{0,4},{4,0},{8,12},{12,8},{16,20},{20,16},{24,28},{28,24},{1,5},{5... | collective-permute-start | bytes 442376 | tf_op jit(solution)/shard_map/ppermute | solution.py:123
  531.9 4.8 collective-permute-start.14
  532.1 11.2 %collective-permute-start.36 = (bf16[384,384]{1,0:T(8,128)(2,1)S(1)}, bf16[384,384]{1,0:T(8,128)(2,1)S(1)}, u32[]{:S(2)}, u32[]{:S(2)}) collective-permute-start(bf16[384,384]{1,0:T(8,128)(2,1)S(1)} %pad_maximum_fusion.11), channel_id=1, source_target_pairs={{0,2},{2,0},{1,3},{3,1},{4,6},{6,4},{5,7},{7,5},{8,10},{10,8},{9,1... | collective-permute-start | bytes 884744 | tf_op jit(solution)/shard_map/ppermute | solution.py:123
  536.8 5.8 collective-permute-start.15
  538.6 17.4 %collective-permute-start.26 = (bf16[384,384]{1,0:T(8,128)(2,1)S(1)}, bf16[384,384]{1,0:T(8,128)(2,1)S(1)}, u32[]{:S(2)}, u32[]{:S(2)}) collective-permute-start(bf16[384,384]{1,0:T(8,128)(2,1)S(1)} %pad_maximum_fusion.10), channel_id=1, source_target_pairs={{0,2},{2,0},{1,3},{3,1},{4,6},{6,4},{5,7},{7,5},{8,10},{10,8},{9,1... | collective-permute-start | bytes 884744 | tf_op jit(solution)/shard_map/ppermute | solution.py:123
  542.8 15.4 %collective-permute-start.16 = (bf16[768,384]{1,0:T(8,128)(2,1)S(1)}, bf16[768,384]{1,0:T(8,128)(2,1)S(1)}, u32[]{:S(2)}, u32[]{:S(2)}) collective-permute-start(bf16[768,384]{1,0:T(8,128)(2,1)S(1)} %pad_maximum_fusion.6), channel_id=1, source_target_pairs={{0,4},{4,0},{8,12},{12,8},{16,20},{20,16},{24,28},{28,24},{1,5},{5... | collective-permute-start | bytes 1769480 | tf_op jit(solution)/shard_map/ppermute | solution.py:123
  544.3 25.9 %collective-permute-start.37 = (bf16[768,384]{1,0:T(8,128)(2,1)}, bf16[768,384]{1,0:T(8,128)(2,1)}, u32[]{:S(2)}, u32[]{:S(2)}) collective-permute-start(bf16[768,384]{1,0:T(8,128)(2,1)} %pad_maximum_fusion.8), channel_id=1, source_target_pairs={{0,1},{1,0},{2,3},{3,2},{4,5},{5,4},{6,7},{7,6},{8,9},{9,8},{10,11... | collective-permute-start | bytes 1769480 | tf_op jit(solution)/shard_map/ppermute | solution.py:123
  556.9 17.7 %collective-permute-start.27 = (bf16[768,384]{1,0:T(8,128)(2,1)}, bf16[768,384]{1,0:T(8,128)(2,1)}, u32[]{:S(2)}, u32[]{:S(2)}) collective-permute-start(bf16[768,384]{1,0:T(8,128)(2,1)} %pad_maximum_fusion.7), channel_id=1, source_target_pairs={{0,1},{1,0},{2,3},{3,2},{4,5},{5,4},{6,7},{7,6},{8,9},{9,8},{10,11... | collective-permute-start | bytes 1769480 | tf_op jit(solution)/shard_map/ppermute | solution.py:123
  559.6 23.8 %collective-permute-start.17 = (bf16[1536,384]{1,0:T(8,128)(2,1)}, bf16[1536,384]{1,0:T(8,128)(2,1)}, u32[]{:S(2)}, u32[]{:S(2)}) collective-permute-start(bf16[1536,384]{1,0:T(8,128)(2,1)} %pad_maximum_fusion.3), channel_id=1, source_target_pairs={{0,1},{1,0},{2,3},{3,2},{4,5},{5,4},{6,7},{7,6},{8,9},{9,8},{10,11... | collective-permute-start | bytes 3538952 | tf_op jit(solution)/shard_map/ppermute | solution.py:123
  (67 other events, 705.6 us)
Sparse Core Ops, SparseCore 0:
  300.6 48.5 reduce-scatter.2
  351.9 47.8 reduce-scatter.4
